TPU v7x, 512 devices: a whole 4x8x8 slice. The times are simulated.
512 devices in a mesh: pool: 64 (over x, z, core), tp: 8 (over y).
Axes of the slice: x: 4, y: 8, z: 8, core: 2. Of those that a mesh axis runs over, the one named last changes fastest.
Arguments:
- prefill_page_pool: bfloat16 [4096, 2, 64, 1024], P('pool', None, None, 'tp'), may hold values from -6 to 6
- prefill_page_table: int32 [2048, 2], P('pool'), may hold values from 0 to 63, as said below
- prefill_length: int32 [2048], P('pool'), may hold values from 1 to 128, as said below
- prefill_target_group: int32 [2048], P('pool'), may hold values from 0 to 63, as said below
- resident_page_pool: bfloat16 [1024, 2, 64, 1024], P('pool', None, None, 'tp'), may hold values from -6 to 6
- resident_page_table: int32 [512, 2], P('pool'), may hold values from 0 to 15, as said below
- resident_length: int32 [512], P('pool'), may hold values from 1 to 128, as said below
- tokens: bfloat16 [4608, 4, 5120], P('pool', None, 'tp'), may hold values from -6 to 6
- base_query_projection: bfloat16 [4608, 4, 4096], P('pool', None, 'tp'), may hold values from -6 to 6
- fresh_key_value: bfloat16 [4608, 4, 2, 1024], P('pool', None, None, 'tp'), may hold values from -6 to 6
- request_adapter: int32 [4608], P('pool'), may hold values from 0 to 511, as said below
- adapter_store_row: int32 [512], replicated, may hold values from 0 to 511
- shrink_weight: bfloat16 [512, 64, 5120], P('pool', None, 'tp'), may hold values from -0.078125 to 0.078125
- expand_weight: bfloat16 [512, 64, 4096], P('pool', None, 'tp'), may hold values from -0.75 to 0.75
Outputs:
- attn_out: bfloat16 [4608, 4, 4096], P('pool', None, 'tp')
Inputs may be any that keep to these rules, and one draw needn't show every extreme that they name: `prefill_target_group`: the 32 requests of one prefill device go to distinct decode groups; at least one decode group receives a request from every prefill device, while other groups may have empty remote slots (arrived_len = 0). `prefill_page_table`: each prefill device's rows name each of its 64 pages once. `prefill_length`: every prefill device has a request of the largest length. `resident_page_table`: each decode group's rows name each of its 16 pages once. `resident_length`: every decode group has a resident request of the largest length. `request_adapter`: adapter_store_row is a permutation; the adapter in store row w is held by pool index w // 8. Among the 72 slots of one group at most 2 use adapters held by one pool index, and those use one adapter; in every group some pool index serves 2 slots.
All inputs are finite; a program needn't handle non-finite values.
Results may differ from a plain program's by a relative error of at most 0.02.
Values may be sent and summed in bfloat16 or wider, within the bound.
A program may use at most 128 MiB of HBM per device.

v0:
```python
import jax
import jax.numpy as jnp
from jax import lax
from jax.sharding import PartitionSpec as P

HEAD_WIDTH = 128


def attend(queries, cache_pages, fresh_rows, lengths):
    number = queries.shape[0]
    decode_step_count = queries.shape[1]
    key_heads = cache_pages.shape[4] // HEAD_WIDTH
    shared = queries.shape[2] // (key_heads * HEAD_WIDTH)
    cached = cache_pages.shape[1] * cache_pages.shape[3]
    total_len = cached + decode_step_count
    keys_all = jnp.concatenate(
        [cache_pages[:, :, 0].reshape(number, cached, -1), fresh_rows[:, :, 0]], 1
    )
    values_all = jnp.concatenate(
        [cache_pages[:, :, 1].reshape(number, cached, -1), fresh_rows[:, :, 1]], 1
    )
    keys_all = keys_all.reshape(number, total_len, key_heads, HEAD_WIDTH)
    values_all = values_all.reshape(number, total_len, key_heads, HEAD_WIDTH)
    query_heads = queries.reshape(number, decode_step_count, key_heads, shared, HEAD_WIDTH)
    scores = jnp.einsum(
        "nskgd,ntkd->nkgst", query_heads, keys_all, preferred_element_type=jnp.float32
    ) * HEAD_WIDTH ** (-0.5)
    position = jnp.arange(total_len, dtype=jnp.int32)[None, None, :]
    step_ids = jnp.arange(decode_step_count, dtype=jnp.int32)[None, :, None]
    visible = jnp.where(
        position < cached, position < lengths[:, None, None], position - cached <= step_ids
    )
    scores = jnp.where(visible[:, None, None], scores, -jnp.inf)
    highest = jnp.max(scores, axis=-1, keepdims=True)
    weights = jnp.exp(scores - highest)
    weights = (weights / jnp.sum(weights, axis=-1, keepdims=True)).astype(jnp.bfloat16)
    mixed_out = jnp.einsum(
        "nkgst,ntkd->nskgd", weights, values_all, preferred_element_type=jnp.float32
    )
    return mixed_out.reshape(number, decode_step_count, -1)


def body(
    prefill_page_pool,
    prefill_page_table,
    prefill_length,
    prefill_target_group,
    resident_page_pool,
    resident_page_table,
    resident_length,
    tokens,
    base_query_projection,
    fresh_key_value,
    request_adapter,
    adapter_store_row,
    shrink_weight,
    expand_weight,
):
    groups = lax.axis_size("pool")
    total_slot_count = tokens.shape[0]
    decode_step_count = tokens.shape[1]
    stored_factors = shrink_weight.shape[0]
    adapter_rank_width = shrink_weight.shape[1]
    picked_pages = prefill_page_pool[prefill_page_table]
    outgoing = (
        jnp.zeros((groups,) + picked_pages.shape[1:], jnp.bfloat16)
        .at[prefill_target_group]
        .set(picked_pages)
    )
    outgoing_len = jnp.zeros((groups,), jnp.int32).at[prefill_target_group].set(prefill_length)
    arrived, arrived_len = (
        lax.all_to_all(outgoing, "pool", split_axis=0, concat_axis=0, tiled=True),
        lax.all_to_all(outgoing_len, "pool", split_axis=0, concat_axis=0, tiled=True),
    )
    adapter_ids = jnp.arange(adapter_store_row.shape[0], dtype=jnp.int32)
    adapter_store_index = jnp.sum(
        jnp.where(request_adapter[:, None] == adapter_ids[None, :], adapter_store_row[None, :], 0),
        axis=1,
    )
    holder = adapter_store_index // stored_factors
    within = adapter_store_index % stored_factors
    owned_by = holder[:, None] == jnp.arange(groups, dtype=jnp.int32)[None, :]
    wanted = jnp.max(jnp.where(owned_by, within[:, None], -1), axis=0)
    asked_row = lax.all_to_all(wanted[:, None], "pool", split_axis=0, concat_axis=0, tiled=True)[
        :, 0
    ]
    clipped_length = jnp.clip(asked_row, 0, stored_factors - 1)
    present_mask = (asked_row >= 0)[:, None, None]
    shrink_factor = jnp.where(present_mask, shrink_weight[clipped_length], 0)
    expand_factor = jnp.where(present_mask, expand_weight[clipped_length], 0)
    got_shrink = lax.all_to_all(
        shrink_factor[:, None], "pool", split_axis=0, concat_axis=0, tiled=True
    )
    got_expand = lax.all_to_all(
        expand_factor[:, None], "pool", split_axis=0, concat_axis=0, tiled=True
    )
    flat_shrink = got_shrink.reshape(groups * adapter_rank_width, -1)
    partial_value = lax.dot_general(
        tokens.reshape(total_slot_count * decode_step_count, -1),
        flat_shrink,
        (((1,), (1,)), ((), ())),
        preferred_element_type=jnp.float32,
    )
    partial_value = partial_value.reshape(
        total_slot_count, decode_step_count, groups, adapter_rank_width
    )
    own_part = jnp.sum(jnp.where(owned_by[:, None, :, None], partial_value, 0.0), axis=2)
    rank_product = lax.psum(own_part.astype(jnp.bfloat16), "tp")
    spread = jnp.where(owned_by[:, None, :, None], rank_product[:, :, None, :], 0)
    spread = spread.reshape(total_slot_count * decode_step_count, groups * adapter_rank_width)
    adapter_delta = jnp.dot(
        spread,
        got_expand.reshape(groups * adapter_rank_width, -1),
        preferred_element_type=jnp.float32,
    )
    adapter_delta = adapter_delta.astype(jnp.bfloat16).reshape(
        total_slot_count, decode_step_count, -1
    )
    query_row_block = (
        base_query_projection.astype(jnp.float32) + adapter_delta.astype(jnp.float32)
    ).astype(jnp.bfloat16)
    resident = resident_page_pool[resident_page_table]
    lengths = jnp.concatenate([resident_length, arrived_len])
    all_pages = jnp.concatenate([resident, arrived], 0)
    mixed_out = attend(query_row_block, all_pages, fresh_key_value, lengths)
    return jnp.where((lengths > 0)[:, None, None], mixed_out, 0.0).astype(jnp.bfloat16)


def solution(mesh):
    return jax.shard_map(
        body,
        mesh=mesh,
        in_specs=(
            P("pool", None, None, "tp"),
            P("pool", None),
            P("pool"),
            P("pool"),
            P("pool", None, None, "tp"),
            P("pool", None),
            P("pool"),
            P("pool", None, "tp"),
            P("pool", None, "tp"),
            P("pool", None, None, "tp"),
            P("pool"),
            P(),
            P("pool", None, "tp"),
            P("pool", None, "tp"),
        ),
        out_specs=P("pool", None, "tp"),
        check_vma=False,
    )
```

profile of v0, /device:TPU:1, one launch (start us, length us, event | category | flops | bytes accessed | tf_op | source)
XLA Modules:
  0.0 385.7 jit_solution(10980120908856883848)
XLA Ops:
  0.0 0.0 copy-start
  0.0 1.0 select_reduce_fusion.1
  1.0 0.1 select_reduce_fusion.2
  1.1 0.7 copy.46
  1.9 14.8 %all-to-all-start.2 = ((s32[64,1,1]{2,1,0:T(1,128)}), s32[64,1,1]{2,1,0:T(1,128)S(1)}, u32[]{:S(2)}, u32[]{:S(2)}) async-start(s32[64,1,1]{2,1,0:T(1,128)} %copy.46), calls=%async_computation.2 | async-start | bytes 65536 | tf_op jit(solution)/shard_map/all_to_all | solution.py:84
  16.7 0.7 compare_select_fusion
  17.4 0.7 compare_select_fusion.3
  18.1 0.1 copy.43
  18.1 0.1 reshape.245
  18.2 0.8 scatter_custom_fusion
  19.1 0.7 copy.41
  19.8 6.2 %all-to-all-done.2 = s32[64,1,1]{2,1,0:T(1,128)S(1)} async-done(((s32[64,1,1]{2,1,0:T(1,128)}), s32[64,1,1]{2,1,0:T(1,128)S(1)}, u32[]{:S(2)}, u32[]{:S(2)}) %all-to-all-start.2) | async-done | bytes 288 | tf_op jit(solution)/shard_map/all_to_all | solution.py:84
  25.9 4.6 %all-to-all-start = ((s32[64,1,1]{2,1,0:T(1,128)}), s32[64,1,1]{2,1,0:T(1,128)S(1)}, u32[]{:S(2)}, u32[]{:S(2)}) async-start(s32[64,1,1]{2,1,0:T(1,128)} %copy.41), calls=%async_computation | async-start | bytes 65536 | tf_op jit(solution)/shard_map/all_to_all | solution.py:73
  30.6 0.0 copy-done
  30.6 2.1 gather_fusion.1
  32.7 3.0 broadcast_in_dim.166
  35.7 0.0 copy-done.4
  35.7 5.4 %scatter_fusion = bf16[64,2,2,64,128]{4,3,2,1,0:T(8,128)(2,1)} fusion(bf16[64,2,2,64,128]{4,3,2,1,0:T(8,128)(2,1)} %broadcast_in_dim.166, s32[32]{0:T(128)S(1)} %compare_select_fusion.3, bf16[32,2,2,64,128]{4,3,2,1,0:T(8,128)(2,1)S(1)} %bitcast.73), kind=kCustom, calls=%fused_computation.5 | custom fusion | bytes 6291584 | tf_op jit(solution)/shard_map/scatter | solution.py:68
  41.2 0.0 all-to-all-done
  41.2 10.7 %all-to-all-start.1 = ((bf16[64,2,2,64,128]{4,3,2,1,0:T(8,128)(2,1)}), bf16[64,2,2,64,128]{4,3,2,1,0:T(8,128)(2,1)}, u32[]{:S(2)}, u32[]{:S(2)}) async-start(bf16[64,2,2,64,128]{4,3,2,1,0:T(8,128)(2,1)} %scatter_fusion), calls=%async_computation.1 | async-start | bytes 8388608 | tf_op jit(solution)/shard_map/all_to_all | solution.py:72
  51.9 1.2 clamp_reduce_fusion
  53.1 0.0 copy-done.2
  53.1 3.5 gather_fusion.2
  56.7 1.2 compare_reduce_fusion
  57.9 5.4 %bitcast_select_fusion = bf16[64,1,64,640]{3,2,1,0:T(8,128)(2,1)} fusion(bf16[64,64,640]{2,1,0:T(8,128)(2,1)} %gather_fusion.2, pred[64]{0:T(512)(128)(4,1)S(1)} %compare_reduce_fusion), kind=kLoop, calls=%fused_computation.8 | loop fusion | flops 2621440 | bytes 10485824 | tf_op jit(solution)/shard_map/jit(_where)/select_n | solution.py:89
  63.3 84.5 %all-to-all-done.1 = bf16[64,2,2,64,128]{4,3,2,1,0:T(8,128)(2,1)} async-done(((bf16[64,2,2,64,128]{4,3,2,1,0:T(8,128)(2,1)}), bf16[64,2,2,64,128]{4,3,2,1,0:T(8,128)(2,1)}, u32[]{:S(2)}, u32[]{:S(2)}) %all-to-all-start.1) | async-done | bytes 4194336 | tf_op jit(solution)/shard_map/all_to_all | solution.py:72
  147.8 6.0 %all-to-all-start.3 = ((bf16[64,1,64,640]{3,2,1,0:T(8,128)(2,1)}), bf16[64,1,64,640]{3,2,1,0:T(8,128)(2,1)}, u32[]{:S(2)}, u32[]{:S(2)}) async-start(bf16[64,1,64,640]{3,2,1,0:T(8,128)(2,1)} %bitcast_select_fusion), calls=%async_computation.3 | async-start | bytes 10485760 | tf_op jit(solution)/shard_map/all_to_all | solution.py:91
  153.8 0.0 copy-done.3
  153.8 2.8 gather_fusion.3
  156.7 4.6 %bitcast_select_fusion.1 = bf16[64,1,64,512]{3,2,1,0:T(8,128)(2,1)} fusion(bf16[64,64,512]{2,1,0:T(8,128)(2,1)} %gather_fusion.3, pred[64]{0:T(512)(128)(4,1)S(1)} %compare_reduce_fusion), kind=kLoop, calls=%fused_computation.12 | loop fusion | flops 2097152 | bytes 8388672 | tf_op jit(solution)/shard_map/jit(_where)/select_n | solution.py:90
  161.3 110.9 %all-to-all-done.3 = bf16[64,1,64,640]{3,2,1,0:T(8,128)(2,1)} async-done(((bf16[64,1,64,640]{3,2,1,0:T(8,128)(2,1)}), bf16[64,1,64,640]{3,2,1,0:T(8,128)(2,1)}, u32[]{:S(2)}, u32[]{:S(2)}) %all-to-all-start.3) | async-done | bytes 5242912 | tf_op jit(solution)/shard_map/all_to_all | solution.py:91
  272.2 6.0 %all-to-all-start.4 = ((bf16[64,1,64,512]{3,2,1,0:T(8,128)(2,1)}), bf16[64,1,64,512]{3,2,1,0:T(8,128)(2,1)}, u32[]{:S(2)}, u32[]{:S(2)}) async-start(bf16[64,1,64,512]{3,2,1,0:T(8,128)(2,1)} %bitcast_select_fusion.1), calls=%async_computation.4 | async-start | bytes 8388608 | tf_op jit(solution)/shard_map/all_to_all | solution.py:94
  278.2 0.0 copy-done.8
  278.2 0.0 copy-start.11
  278.2 0.1 reshape.228
  278.3 0.0 copy-done.10
  278.3 0.1 copy.42
  278.4 0.1 reshape.237
  278.5 0.2 fusion.20
  278.8 0.6 gather_fusion
  279.5 0.1 iota_compare_fusion.2
  279.6 1.2 reduce.2
  280.8 0.1 broadcast_compare_fusion
  280.9 0.1 iota_compare_fusion.1
  281.0 0.1 broadcast_select_fusion.1
  281.1 4.0 %pad_maximum_fusion = (bf16[72,2,1,64,128]{4,3,2,1,0:T(8,128)(2,1)}, bf16[72,2,1,64,128]{4,3,2,1,0:T(8,128)(2,1)}) fusion(bf16[64,2,2,64,128]{4,3,2,1,0:T(8,128)(2,1)} %all-to-all-done.1, bf16[8,2,2,64,128]{4,3,2,1,0:T(8,128)(2,1)S(1)} %bitcast.76), kind=kLoop, calls=%fused_computation.20 | loop fusion | flops 2359296 | bytes 9437184 | tf_op jit(solution)/shard_map/concatenate | solution.py:124
  285.1 6.7 %convolution_bitcast_fusion = f32[288,4096]{1,0:T(8,128)} fusion(bf16[4096,640]{1,0:T(8,128)(2,1)} %bitcast.14, bf16[288,640]{1,0:T(8,128)(2,1)S(1)} %reshape.228), kind=kOutput, calls=%fused_computation.7 | convolution fusion | flops 1509949440 | bytes 10330112 | tf_op jit(solution)/shard_map/dot_general | solution.py:98
  291.8 8.5 %reshape.229 = f32[72,4,64,64]{3,2,1,0:T(8,128)} reshape(f32[288,4096]{1,0:T(8,128)} %convolution_bitcast_fusion) | data formatting | bytes 9437184 | tf_op jit(solution)/shard_map/reshape | solution.py:104
  300.4 5.2 %select_reduce_fusion = bf16[72,4,64]{2,1,0:T(4,128)(2,1)S(1)} fusion(f32[72,4,64,64]{3,2,1,0:T(8,128)} %reshape.229, pred[72,64]{1,0:T(8,128)(4,1)S(1)} %iota_compare_fusion.2), kind=kLoop, calls=%fused_computation.6 | loop fusion | flops 2340864 | bytes 4760064 | tf_op jit(solution)/shard_map/reduce_sum | solution.py:107
  305.5 27.3 %psum.7 = bf16[72,4,64]{2,1,0:T(4,128)(2,1)S(1)} all-reduce(bf16[72,4,64]{2,1,0:T(4,128)(2,1)S(1)} %select_reduce_fusion), channel_id=1, replica_groups=mesh['pool'=64,'tp'=8] {'tp'}, use_global_device_ids=true, to_apply=%region_5.6 | all-reduce | flops 18432 | bytes 73728 | tf_op jit(solution)/shard_map/psum | solution.py:108
  332.8 2.9 broadcast_select_fusion
  335.7 7.1 %select_n.117 = bf16[288,4096]{1,0:T(8,128)(2,1)} reshape(bf16[72,4,64,64]{3,2,1,0:T(8,128)(2,1)} %broadcast_select_fusion) | data formatting | bytes 4718592 | tf_op jit(solution)/shard_map/jit(_where)/select_n | solution.py:109
  342.8 31.3 %all-to-all-done.4 = bf16[64,1,64,512]{3,2,1,0:T(8,128)(2,1)} async-done(((bf16[64,1,64,512]{3,2,1,0:T(8,128)(2,1)}), bf16[64,1,64,512]{3,2,1,0:T(8,128)(2,1)}, u32[]{:S(2)}, u32[]{:S(2)}) %all-to-all-start.4) | async-done | bytes 4194336 | tf_op jit(solution)/shard_map/all_to_all | solution.py:94
  374.1 4.3 %fusion.8 = f32[288,512]{1,0:T(8,128)S(1)} fusion(bf16[288,4096]{1,0:T(8,128)(2,1)} %select_n.117, bf16[4096,512]{1,0:T(8,128)(2,1)} %bitcast.17), kind=kOutput, calls=%fused_computation.25 | convolution fusion | flops 1208254464 | bytes 7143424 | tf_op jit(solution)/shard_map/dot_general | solution.py:111
  378.4 0.2 reshape.234
  378.6 0.2 add_convert_fusion
  378.7 0.1 reshape.231
  378.9 3.5 fusion.21
  382.4 0.0 copy-start.5
  382.4 0.9 fusion.12
  383.3 0.8 fusion.14
  384.1 0.0 copy-start.1
  384.1 1.5 fusion.11
  385.6 0.1 copy-done.1
  (24 shorter events, 0.1 us)
Async XLA Ops:
  0.0 30.6 %copy-start = (bf16[64,2,64,128]{3,2,1,0:T(8,128)(2,1)S(1)}, bf16[64,2,64,128]{3,2,1,0:T(8,128)(2,1)}, u32[]{:S(2)}) copy-start(bf16[64,2,64,128]{3,2,1,0:T(8,128)(2,1)} %param.14) | copy-start | bytes 6291460
  1.9 24.1 %all-to-all-start.2 = ((s32[64,1,1]{2,1,0:T(1,128)}), s32[64,1,1]{2,1,0:T(1,128)S(1)}, u32[]{:S(2)}, u32[]{:S(2)}) async-start(s32[64,1,1]{2,1,0:T(1,128)} %copy.46), calls=%async_computation.2 | async-start | bytes 65536 | tf_op jit(solution)/shard_map/all_to_all | solution.py:84
  25.9 15.2 %all-to-all-start = ((s32[64,1,1]{2,1,0:T(1,128)}), s32[64,1,1]{2,1,0:T(1,128)S(1)}, u32[]{:S(2)}, u32[]{:S(2)}) async-start(s32[64,1,1]{2,1,0:T(1,128)} %copy.41), calls=%async_computation | async-start | bytes 65536 | tf_op jit(solution)/shard_map/all_to_all | solution.py:73
  32.7 3.0 copy-start.4
  41.2 12.0 %copy-start.2 = (bf16[8,64,640]{2,1,0:T(8,128)(2,1)S(1)}, bf16[8,64,640]{2,1,0:T(8,128)(2,1)}, u32[]{:S(2)}) copy-start(bf16[8,64,640]{2,1,0:T(8,128)(2,1)} %param.26) | copy-start | bytes 1966084
  41.2 106.6 %all-to-all-start.1 = ((bf16[64,2,2,64,128]{4,3,2,1,0:T(8,128)(2,1)}), bf16[64,2,2,64,128]{4,3,2,1,0:T(8,128)(2,1)}, u32[]{:S(2)}, u32[]{:S(2)}) async-start(bf16[64,2,2,64,128]{4,3,2,1,0:T(8,128)(2,1)} %scatter_fusion), calls=%async_computation.1 | async-start | bytes 8388608 | tf_op jit(solution)/shard_map/all_to_all | solution.py:72
  147.8 6.1 %copy-start.3 = (bf16[8,64,512]{2,1,0:T(8,128)(2,1)S(1)}, bf16[8,64,512]{2,1,0:T(8,128)(2,1)}, u32[]{:S(2)}) copy-start(bf16[8,64,512]{2,1,0:T(8,128)(2,1)} %param.27) | copy-start | bytes 1572868
  147.8 124.4 %all-to-all-start.3 = ((bf16[64,1,64,640]{3,2,1,0:T(8,128)(2,1)}), bf16[64,1,64,640]{3,2,1,0:T(8,128)(2,1)}, u32[]{:S(2)}, u32[]{:S(2)}) async-start(bf16[64,1,64,640]{3,2,1,0:T(8,128)(2,1)} %bitcast_select_fusion), calls=%async_computation.3 | async-start | bytes 10485760 | tf_op jit(solution)/shard_map/all_to_all | solution.py:91
  161.2 117.0 %copy-start.8 = (bf16[72,4,640]{2,1,0:T(4,128)(2,1)S(1)}, bf16[72,4,640]{2,1,0:T(4,128)(2,1)}, u32[]{:S(2)}) copy-start(bf16[72,4,640]{2,1,0:T(4,128)(2,1)} %param.21) | copy-start | bytes 1105924
  161.2 117.1 %copy-start.10 = (s32[8,2]{0,1:T(2,128)S(1)}, s32[8,2]{0,1:T(2,128)}, u32[]{:S(2)}) copy-start(s32[8,2]{0,1:T(2,128)} %param.19) | copy-start | bytes 196
  161.2 117.3 %copy-start.6 = (bf16[72,4,2,128]{3,2,1,0:T(2,128)(2,1)S(1)}, bf16[72,4,2,128]{3,2,1,0:T(2,128)(2,1)}, u32[]{:S(2)}) copy-start(bf16[72,4,2,128]{3,2,1,0:T(2,128)(2,1)} %param.23) | copy-start | bytes 442372
  161.3 117.6 %copy-start.7 = (bf16[16,2,64,128]{3,2,1,0:T(8,128)(2,1)S(1)}, bf16[16,2,64,128]{3,2,1,0:T(8,128)(2,1)}, u32[]{:S(2)}) copy-start(bf16[16,2,64,128]{3,2,1,0:T(8,128)(2,1)} %param.18) | copy-start | bytes 1572868
  272.2 101.9 %all-to-all-start.4 = ((bf16[64,1,64,512]{3,2,1,0:T(8,128)(2,1)}), bf16[64,1,64,512]{3,2,1,0:T(8,128)(2,1)}, u32[]{:S(2)}, u32[]{:S(2)}) async-start(bf16[64,1,64,512]{3,2,1,0:T(8,128)(2,1)} %bitcast_select_fusion.1), calls=%async_computation.4 | async-start | bytes 8388608 | tf_op jit(solution)/shard_map/all_to_all | solution.py:94
  278.2 2.6 copy-start.11
  374.1 4.5 %copy-start.9 = (bf16[72,4,512]{2,1,0:T(4,128)(2,1)S(1)}, bf16[72,4,512]{2,1,0:T(4,128)(2,1)}, u32[]{:S(2)}) copy-start(bf16[72,4,512]{2,1,0:T(4,128)(2,1)} %param.22) | copy-start | bytes 884740
  382.4 1.7 copy-start.5
  384.1 1.6 copy-start.1
where the time goes:
time: 387 us; the launch traced here: 386 us
  waiting for transfers between devices  233 us (60%)
  starting transfers between devices  42.2 us (11%)
  local copies, waits for them, and re-layouts  36.6 us (9%)
  other arithmetic  30.3 us (8%)
  blocking collectives  27.3 us (7%)
  matrix products  16.1 us (4%)
    all_to_all x1, waiting for transfers between devices, body(): lax.all_to_all(shrink_factor[:, None], 'pool', split_axis=0, concat_axis=...  111 us
    all_to_all x1, waiting for transfers between devices, body(): lax.all_to_all(outgoing, 'pool', split_axis=0, concat_axis=0, tiled=True)  84.5 us
    all_to_all x1, waiting for transfers between devices, body(): lax.all_to_all(expand_factor[:, None], 'pool', split_axis=0, concat_axis=...  31.3 us
    psum x1, blocking collectives, body(): rank_product = lax.psum(own_part.astype(jnp.bfloat16), 'tp')  27.3 us
    all_to_all x1, starting transfers between devices, body(): lax.all_to_all(wanted[:, None], 'pool', split_axis=0, concat_axis=0, tile...  14.8 us
    all_to_all x1, starting transfers between devices, body(): lax.all_to_all(outgoing, 'pool', split_axis=0, concat_axis=0, tiled=True)  10.7 us
    reshape x1, local copies, waits for them, and re-layouts, body(): partial_value.reshape(total_slot_count, decode_step_count, groups, adapte...  8.54 us
  transfers between devices with their start and end apart: 5, of which 4 were waited for; matrix products, arithmetic and copies ran while one was open for 18% of the time, Pallas kernels for 0%

commit v1 on v0

v1 whole, which is shorter than its diff:
```python
import jax
import jax.numpy as jnp
from jax import lax
from jax.sharding import PartitionSpec as P

HEAD_WIDTH = 128
SCALE = HEAD_WIDTH ** (-0.5)


def partial_attend(queries, keys, values, visible):
    scores = (
        jnp.einsum("nshd,ntd->nsht", queries, keys, preferred_element_type=jnp.float32) * SCALE
    )
    scores = jnp.where(visible[:, :, None, :], scores, -jnp.inf)
    highest = jnp.max(scores, axis=-1, keepdims=True)
    weights = jnp.exp(scores - highest)
    total = jnp.sum(weights, axis=-1, keepdims=True)
    mixed = jnp.einsum(
        "nsht,ntd->nshd", weights.astype(jnp.bfloat16), values, preferred_element_type=jnp.float32
    )
    return mixed / total, highest + jnp.log(total)


def body(
    prefill_page_pool,
    prefill_page_table,
    prefill_length,
    prefill_target_group,
    resident_page_pool,
    resident_page_table,
    resident_length,
    tokens,
    base_query_projection,
    fresh_key_value,
    request_adapter,
    adapter_store_row,
    shrink_weight,
    expand_weight,
):
    groups = lax.axis_size("pool")
    slots, steps, width = tokens.shape
    stored, rank, _ = shrink_weight.shape
    out_width = expand_weight.shape[2]
    heads = out_width // HEAD_WIDTH
    resident = resident_length.shape[0]
    per_owner = 2

    adapter_ids = jnp.arange(adapter_store_row.shape[0], dtype=jnp.int32)
    store_index = jnp.sum(
        jnp.where(request_adapter[:, None] == adapter_ids[None, :], adapter_store_row[None, :], 0),
        axis=1,
    )
    holder = store_index // stored
    within = store_index % stored
    slot_ids = jnp.arange(slots, dtype=jnp.int32)
    earlier = (holder[:, None] == holder[None, :]) & (slot_ids[None, :] < slot_ids[:, None])
    place = holder * per_owner + jnp.sum(earlier.astype(jnp.int32), axis=1)
    places = groups * per_owner
    dispatch = (jnp.arange(places, dtype=jnp.int32)[:, None] == place[None, :]).astype(jnp.bfloat16)
    owned_by = holder[:, None] == jnp.arange(groups, dtype=jnp.int32)[None, :]
    wanted = jnp.max(jnp.where(owned_by, within[:, None], 0), axis=0)

    asked = lax.all_to_all(wanted[:, None], "pool", 0, 0, tiled=True)[:, 0]
    outgoing = jnp.dot(
        dispatch, tokens.reshape(slots, steps * width), preferred_element_type=jnp.float32
    ).astype(jnp.bfloat16)
    visiting = lax.all_to_all(outgoing, "pool", 0, 0, tiled=True)
    rows = places * steps
    visiting = visiting.reshape(rows, width)
    which = jnp.repeat(asked, per_owner * steps)
    chosen = which[:, None] == jnp.arange(stored * rank, dtype=jnp.int32)[None, :] // rank
    every = lax.dot_general(
        visiting,
        shrink_weight.reshape(stored * rank, width),
        (((1,), (1,)), ((), ())),
        preferred_element_type=jnp.float32,
    )
    low = jnp.sum(jnp.where(chosen, every, 0.0).reshape(rows, stored, rank), axis=1)
    low = lax.psum(low.astype(jnp.bfloat16), "tp")
    spread = jnp.where(chosen, jnp.tile(low, (1, stored)), 0)
    delta = jnp.dot(
        spread, expand_weight.reshape(stored * rank, out_width), preferred_element_type=jnp.float32
    ).astype(jnp.bfloat16)
    delta = lax.all_to_all(
        delta.reshape(places, steps * out_width), "pool", 0, 0, tiled=True
    )
    delta = lax.dot_general(
        dispatch, delta, (((0,), (0,)), ((), ())), preferred_element_type=jnp.float32
    )
    query = (
        base_query_projection.astype(jnp.float32) + delta.reshape(slots, steps, out_width)
    ).astype(jnp.bfloat16)

    arrived = lax.all_to_all(query[resident:], "pool", 0, 0, tiled=True)
    arrived = arrived[prefill_target_group].reshape(-1, steps, heads, HEAD_WIDTH)
    pages = prefill_page_pool[prefill_page_table]
    cached = pages.shape[1] * pages.shape[3]
    position = jnp.arange(cached, dtype=jnp.int32)[None, None, :]
    keys = pages[:, :, 0].reshape(-1, cached, HEAD_WIDTH)
    values = pages[:, :, 1].reshape(-1, cached, HEAD_WIDTH)
    mixed, level = partial_attend(
        arrived, keys, values, position < prefill_length[:, None, None]
    )
    number = mixed.shape[0]
    back = (
        jnp.zeros((groups, steps * out_width), jnp.bfloat16)
        .at[prefill_target_group]
        .set(mixed.astype(jnp.bfloat16).reshape(number, -1))
    )
    back_level = (
        jnp.full((groups, steps * heads), -jnp.inf, jnp.float32)
        .at[prefill_target_group]
        .set(level.reshape(number, -1))
    )
    back = lax.all_to_all(back, "pool", 0, 0, tiled=True)
    back_level = lax.all_to_all(back_level, "pool", 0, 0, tiled=True)

    query = query.reshape(slots, steps, heads, HEAD_WIDTH)
    own_pages = resident_page_pool[resident_page_table]
    own_mixed, own_level = partial_attend(
        query[:resident],
        own_pages[:, :, 0].reshape(-1, cached, HEAD_WIDTH),
        own_pages[:, :, 1].reshape(-1, cached, HEAD_WIDTH),
        position < resident_length[:, None, None],
    )
    step_ids = jnp.arange(steps, dtype=jnp.int32)
    fresh_mixed, fresh_level = partial_attend(
        query,
        fresh_key_value[:, :, 0],
        fresh_key_value[:, :, 1],
        (step_ids[None, :] <= step_ids[:, None])[None],
    )
    cache_mixed = jnp.concatenate(
        [own_mixed, back.reshape(-1, steps, heads, HEAD_WIDTH).astype(jnp.float32)], 0
    )
    cache_level = jnp.concatenate(
        [own_level, back_level.reshape(-1, steps, heads, 1)], 0
    )
    top = jnp.maximum(cache_level, fresh_level)
    cache_share = jnp.exp(cache_level - top)
    fresh_share = jnp.exp(fresh_level - top)
    result = (cache_share * cache_mixed + fresh_share * fresh_mixed) / (cache_share + fresh_share)
    result = jnp.where(cache_level > -jnp.inf, result, 0.0)
    return result.reshape(slots, steps, out_width).astype(jnp.bfloat16)


def solution(mesh):
    return jax.shard_map(
        body,
        mesh=mesh,
        in_specs=(
            P("pool", None, None, "tp"),
            P("pool", None),
            P("pool"),
            P("pool"),
            P("pool", None, None, "tp"),
            P("pool", None),
            P("pool"),
            P("pool", None, "tp"),
            P("pool", None, "tp"),
            P("pool", None, None, "tp"),
            P("pool"),
            P(),
            P("pool", None, "tp"),
            P("pool", None, "tp"),
        ),
        out_specs=P("pool", None, "tp"),
        check_vma=False,
    )
```

time: 387 us -> 250 us (0.65)
  waiting for transfers between devices: 233 us -> 115 us
  blocking collectives: 27.3 us -> 0 us
  other arithmetic: 30.3 us -> 9.39 us
  starting transfers between devices: 42.2 us -> 58.4 us
  between operations: 0.36 us -> 13.8 us
    all_to_all x5 -> x6, waiting for transfers between devices: 233 us -> 46.3 us  [the longest x1 17 us: body(): visiting = lax.all_to_all(outgoing, 'pool', 0, 0, tiled=True)]
    psum x0 -> x1, waiting for transfers between devices: none -> 68.8 us  [body(): low = lax.psum(low.astype(jnp.bfloat16), 'tp')]
    psum x1 -> x0, blocking collectives: 27.3 us -> none  [body(): rank_product = lax.psum(own_part.astype(jnp.bfloat16), 'tp')]
    all_to_all x5 -> x6, starting transfers between devices: 42.2 us -> 58.3 us  [the longest x1 16 us: body(): lax.all_to_all(delta.reshape(places, steps * out_width), 'pool', 0, 0, ti...]
    select_n x9 -> x6, other arithmetic: 14.3 us -> 0.04 us  [the longest x1 0.01 us: body(): holder = store_index // stored]
    select_n x3 -> x2, local copies, waits for them, and re-layouts: 7.32 us -> 0.17 us  [the longest x1 0.09 us: body(): pages = prefill_page_pool[prefill_page_table]]
    slice x1 -> x6, local copies, waits for them, and re-layouts: 0.21 us -> 7.21 us  [the longest x1 2.78 us: body(): keys = pages[:, :, 0].reshape(-1, cached, HEAD_WIDTH)]
    all_to_all x2 -> x7, local copies, waits for them, and re-layouts: 1.41 us -> 7.46 us  [the longest x3 5.09 us: body(): lax.all_to_all(delta.reshape(places, steps * out_width), 'pool', 0, 0, ti...]
  transfers between devices with their start and end apart: 5 -> 7, of which waited for: 4 -> 6; matrix products, arithmetic and copies ran while one was open for 18% -> 13% of each run, Pallas kernels for 0% -> 0%
where the time goes in v1:
time: 250 us; the launch traced here: 249 us
  waiting for transfers between devices  115 us (46%)
  starting transfers between devices  58.4 us (23%)
  local copies, waits for them, and re-layouts  33.2 us (13%)
  matrix products  19.1 us (8%)
  between operations  13.8 us (6%)
  other arithmetic  9.39 us (4%)
    psum x1, waiting for transfers between devices, body(): low = lax.psum(low.astype(jnp.bfloat16), 'tp')  68.8 us
    all_to_all x1, waiting for transfers between devices, body(): visiting = lax.all_to_all(outgoing, 'pool', 0, 0, tiled=True)  17 us
    all_to_all x1, starting transfers between devices, body(): lax.all_to_all(delta.reshape(places, steps * out_width), 'pool', 0, 0, ti...  16 us
    all_to_all x1, starting transfers between devices, body(): asked = lax.all_to_all(wanted[:, None], 'pool', 0, 0, tiled=True)[:, 0]  14.8 us
    all_to_all x1, starting transfers between devices, body(): back_level = lax.all_to_all(back_level, 'pool', 0, 0, tiled=True)  10.3 us
    all_to_all x1, waiting for transfers between devices, body(): back = lax.all_to_all(back, 'pool', 0, 0, tiled=True)  9.88 us
    all_to_all x1, waiting for transfers between devices, body(): lax.all_to_all(delta.reshape(places, steps * out_width), 'pool', 0, 0, ti...  8.6 us
    dot_general x3, matrix products, partial_attend(): jnp.einsum('nshd,ntd->nsht', queries, keys, preferred_element_type=jnp.fl...  7.18 us
  transfers between devices with their start and end apart: 7, of which 6 were waited for; matrix products, arithmetic and copies ran while one was open for 13% of the time, Pallas kernels for 0%

profile of v1, /device:TPU:1, one launch (start us, length us, event | category | flops | bytes accessed | tf_op | source)
XLA Modules:
  0.0 248.9 jit_solution(7605638914947759204)
XLA Ops:
  6.5 1.0 select_reduce_fusion
  7.7 0.7 copy.166
  8.4 14.8 %all-to-all-start = ((s32[64,1,1]{2,1,0:T(1,128)}), s32[64,1,1]{2,1,0:T(1,128)S(1)}, u32[]{:S(2)}, u32[]{:S(2)}) async-start(s32[64,1,1]{2,1,0:T(1,128)} %copy.166), calls=%async_computation | async-start | bytes 65536 | tf_op jit(solution)/shard_map/all_to_all | solution.py:63
  23.3 0.2 convert_reduce_fusion
  23.5 1.0 copy.212
  24.5 0.4 convolution_convert_fusion
  25.0 1.1 all_to_all.37
  26.1 6.4 %all-to-all-done = s32[64,1,1]{2,1,0:T(1,128)S(1)} async-done(((s32[64,1,1]{2,1,0:T(1,128)}), s32[64,1,1]{2,1,0:T(1,128)S(1)}, u32[]{:S(2)}, u32[]{:S(2)}) %all-to-all-start) | async-done | bytes 288 | tf_op jit(solution)/shard_map/all_to_all | solution.py:63
  32.5 4.7 %all-to-all-start.1 = ((bf16[64,2,2560]{2,1,0:T(2,128)(2,1)}), bf16[64,2,2560]{2,1,0:T(2,128)(2,1)S(1)}, u32[]{:S(2)}, u32[]{:S(2)}) async-start(bf16[64,2,2560]{2,1,0:T(2,128)(2,1)} %all_to_all.37), calls=%async_computation.1 | async-start | bytes 1310720 | tf_op jit(solution)/shard_map/all_to_all | solution.py:67
  37.7 0.6 pad_clamp_fusion.1
  38.3 0.7 iota_compare_fusion.6
  39.0 1.2 reduce
  40.4 17.0 %all-to-all-done.1 = bf16[64,2,2560]{2,1,0:T(2,128)(2,1)S(1)} async-done(((bf16[64,2,2560]{2,1,0:T(2,128)(2,1)}), bf16[64,2,2560]{2,1,0:T(2,128)(2,1)S(1)}, u32[]{:S(2)}, u32[]{:S(2)}) %all-to-all-start.1) | async-done | bytes 655392 | tf_op jit(solution)/shard_map/all_to_all | solution.py:67
  57.4 1.0 reshape.355
  58.4 1.9 convolution_select_fusion
  60.3 0.7 reduce_sum.56
  61.0 68.8 %all-reduce.2.cloned.1.call-done = bf16[512,64]{0,1:T(8,128)(2,1)} async-done(((bf16[512,64]{0,1:T(8,128)(2,1)}), bf16[512,64]{0,1:T(8,128)(2,1)}) %all-reduce.2.cloned.1.call-update) | async-done | bytes 65552 | tf_op jit(solution)/shard_map/psum | solution.py:79
  129.8 1.7 fusion
  131.5 1.0 all_to_all.39
  132.5 16.0 %all-to-all-start.2 = ((bf16[64,2,2048]{2,1,0:T(2,128)(2,1)}), bf16[64,2,2048]{2,1,0:T(2,128)(2,1)}, u32[]{:S(2)}, u32[]{:S(2)}) async-start(bf16[64,2,2048]{2,1,0:T(2,128)(2,1)} %all_to_all.39), calls=%async_computation.2 | async-start | bytes 1048576 | tf_op jit(solution)/shard_map/all_to_all | solution.py:84
  148.6 0.6 iota_compare_fusion.7
  149.2 2.2 gather_fusion.2
  151.3 0.6 gather_fusion
  152.0 0.7 iota_compare_fusion.5
  152.7 0.9 fusion.49
  153.6 0.8 fusion.48
  154.4 2.8 %fusion.47 = (bf16[32,2,1,64,128]{4,3,2,1,0:T(8,128)(2,1)S(1)}, bf16[32,2,1,64,128]{4,3,2,1,0:T(8,128)(2,1)}) fusion(bf16[32,2,2,64,128]{4,3,2,1,0:T(8,128)(2,1)} %bitcast.85), kind=kLoop, calls=%fused_computation.102 | loop fusion | bytes 4194304 | tf_op jit(solution)/shard_map/slice | solution.py:99
  157.2 8.6 %all-to-all-done.2 = bf16[64,2,2048]{2,1,0:T(2,128)(2,1)} async-done(((bf16[64,2,2048]{2,1,0:T(2,128)(2,1)}), bf16[64,2,2048]{2,1,0:T(2,128)(2,1)}, u32[]{:S(2)}, u32[]{:S(2)}) %all-to-all-start.2) | async-done | bytes 524320 | tf_op jit(solution)/shard_map/all_to_all | solution.py:84
  165.8 2.0 all_to_all.41
  167.8 2.1 copy.167
  169.9 1.5 fusion.3
  171.4 0.7 slice.44
  172.1 0.8 reshape.359
  172.9 1.9 copy.173
  174.8 6.5 %all-to-all-start.3 = ((bf16[64,4,512]{2,1,0:T(4,128)(2,1)}), bf16[64,4,512]{2,1,0:T(4,128)(2,1)}, u32[]{:S(2)}, u32[]{:S(2)}) async-start(bf16[64,4,512]{2,1,0:T(4,128)(2,1)} %copy.173), calls=%async_computation.3 | async-start | bytes 524288 | tf_op jit(solution)/shard_map/all_to_all | solution.py:94
  181.3 4.5 %fusion.12 = f32[72,4,4,4]{2,3,1,0:T(4,128)} fusion(bf16[72,4,4,128]{3,2,0,1:T(4,128)(2,1)} %reshape.359, bf16[72,4,1,128]{3,2,1,0:T(2,128)(2,1)} %get-tuple-element.13), kind=kOutput, calls=%fused_computation.28 | convolution fusion | flops 1179648 | bytes 387072 | tf_op jit(solution)/shard_map/nshd,ntd->nsht/dot_general | solution.py:12
  185.8 1.3 copy.184
  187.1 1.0 fusion.51
  188.2 0.2 fusion.23
  188.4 0.8 fusion.30
  189.3 0.8 fusion.34
  190.1 0.8 copy.205
  190.9 1.0 copy.196
  191.9 1.8 convolution_divide_fusion.2
  193.8 1.7 gather_fusion.1
  195.5 0.7 reshape.358
  196.2 1.7 fusion.50
  198.0 0.4 fusion.17
  198.6 1.4 scatter_custom_fusion
  200.0 10.3 %all-to-all-start.4 = ((f32[64,1,16]{2,1,0:T(1,128)}), f32[64,1,16]{2,1,0:T(1,128)S(1)}, u32[]{:S(2)}, u32[]{:S(2)}) async-start(f32[64,1,16]{2,1,0:T(1,128)} %bitcast.18), calls=%async_computation.4 | async-start | bytes 65536 | tf_op jit(solution)/shard_map/all_to_all | solution.py:116
  210.3 1.7 fusion.5
  212.1 1.0 scatter_custom_fusion.1
  213.1 0.5 broadcast.269
  213.6 0.7 reduce.1
  214.3 0.9 reshape.422
  215.2 4.4 %all-to-all-done.4 = f32[64,1,16]{2,1,0:T(1,128)S(1)} async-done(((f32[64,1,16]{2,1,0:T(1,128)}), f32[64,1,16]{2,1,0:T(1,128)S(1)}, u32[]{:S(2)}, u32[]{:S(2)}) %all-to-all-start.4) | async-done | bytes 4128 | tf_op jit(solution)/shard_map/all_to_all | solution.py:116
  219.6 5.9 %all-to-all-start.5 = ((bf16[64,2,1024]{2,1,0:T(2,128)(2,1)}), bf16[64,2,1024]{2,1,0:T(2,128)(2,1)S(1)}, u32[]{:S(2)}, u32[]{:S(2)}) async-start(bf16[64,2,1024]{2,1,0:T(2,128)(2,1)} %reshape.422), calls=%async_computation.5 | async-start | bytes 524288 | tf_op jit(solution)/shard_map/all_to_all | solution.py:115
  226.1 0.8 copy.194
  226.9 0.8 copy.197
  227.6 9.9 %all-to-all-done.5 = bf16[64,2,1024]{2,1,0:T(2,128)(2,1)S(1)} async-done(((bf16[64,2,1024]{2,1,0:T(2,128)(2,1)}), bf16[64,2,1024]{2,1,0:T(2,128)(2,1)S(1)}, u32[]{:S(2)}, u32[]{:S(2)}) %all-to-all-start.5) | async-done | bytes 262176 | tf_op jit(solution)/shard_map/all_to_all | solution.py:115
  237.5 0.2 reshape.423
  237.7 0.5 convert_element_type.59
  238.3 3.0 %fusion.9 = bf16[72,4,4,128]{3,2,1,0:T(4,128)(2,1)S(1)} fusion(bf16[72,4,4,4]{3,2,1,0:T(4,128)(2,1)S(1)} %copy-done.4, f32[64,4,4,128]{3,2,1,0:T(4,128)S(1)} %bitcast.94, f32[8,4,4,128]{3,2,1,0:T(4,128)} %convolution_divide_fusion.2, f32[72,4,4]{2,1,0:T(4,128)} %copy.197, f32[72,4,4]{2,1,0:T(4,128)S(1)} %copy-done.5, f32[72,4,4]{2,1,0:T(4,128)} %copy.194, ...), kind=kOutput, calls=%fused_computation.24 | convolution fusion | flops 2359296 | bytes 987264 | tf_op jit(solution)/shard_map/nsht,ntd->nshd/dot_general | solution.py:18
  241.3 0.8 convert_element_type.58
  (57 shorter events, 1.9 us)
Async XLA Ops:
  6.5 142.6 %copy-start = (bf16[64,2,64,128]{3,2,1,0:T(8,128)(2,1)S(1)}, bf16[64,2,64,128]{3,2,1,0:T(8,128)(2,1)}, u32[]{:S(2)}) copy-start(bf16[64,2,64,128]{3,2,1,0:T(8,128)(2,1)} %param.14) | copy-start | bytes 6291460
  8.4 24.1 %all-to-all-start = ((s32[64,1,1]{2,1,0:T(1,128)}), s32[64,1,1]{2,1,0:T(1,128)S(1)}, u32[]{:S(2)}, u32[]{:S(2)}) async-start(s32[64,1,1]{2,1,0:T(1,128)} %copy.166), calls=%async_computation | async-start | bytes 65536 | tf_op jit(solution)/shard_map/all_to_all | solution.py:63
  23.4 13.8 %copy-start.6 = (s32[32,2]{0,1:T(2,128)S(1)}, s32[32,2]{0,1:T(2,128)}, u32[]{:S(2)}) copy-start(s32[32,2]{0,1:T(2,128)} %param.15) | copy-start | bytes 772
  23.5 14.0 %copy-start.7 = (s32[8,2]{0,1:T(2,128)S(1)}, s32[8,2]{0,1:T(2,128)}, u32[]{:S(2)}) copy-start(s32[8,2]{0,1:T(2,128)} %param.19) | copy-start | bytes 196
  23.5 14.2 %copy-start.10 = (s32[32]{0:T(128)S(1)}, s32[32]{0:T(128)}, u32[]{:S(2)}) copy-start(s32[32]{0:T(128)} %param.17) | copy-start | bytes 388
  23.5 14.8 %copy-start.11 = (s32[8]{0:T(128)S(1)}, s32[8]{0:T(128)}, u32[]{:S(2)}) copy-start(s32[8]{0:T(128)} %param.20) | copy-start | bytes 100
  32.5 24.9 %all-to-all-start.1 = ((bf16[64,2,2560]{2,1,0:T(2,128)(2,1)}), bf16[64,2,2560]{2,1,0:T(2,128)(2,1)S(1)}, u32[]{:S(2)}, u32[]{:S(2)}) async-start(bf16[64,2,2560]{2,1,0:T(2,128)(2,1)} %all_to_all.37), calls=%async_computation.1 | async-start | bytes 1310720 | tf_op jit(solution)/shard_map/all_to_all | solution.py:67
  37.2 92.6 %all-reduce.2.cloned.1.call-start = ((), (), s32[]{:S(2)}) async-start(), calls=%async_computation.6 | async-start | bytes 131072 | tf_op jit(solution)/shard_map/psum | solution.py:79
  37.7 2.5 %copy-start.9 = (s32[32]{0:T(128)}, s32[32]{0:T(128)S(1)}, u32[]{:S(2)}) copy-start(s32[32]{0:T(128)S(1)} %compare_select_fusion.4) | copy-start | bytes 388
  132.5 33.3 %all-to-all-start.2 = ((bf16[64,2,2048]{2,1,0:T(2,128)(2,1)}), bf16[64,2,2048]{2,1,0:T(2,128)(2,1)}, u32[]{:S(2)}, u32[]{:S(2)}) async-start(bf16[64,2,2048]{2,1,0:T(2,128)(2,1)} %all_to_all.39), calls=%async_computation.2 | async-start | bytes 1048576 | tf_op jit(solution)/shard_map/all_to_all | solution.py:84
  149.1 2.2 copy-start.3
  149.1 2.8 %copy-start.8 = (s32[32]{0:T(128)S(1)}, s32[32]{0:T(128)}, u32[]{:S(2)}) copy-start(s32[32]{0:T(128)} %param.16) | copy-start | bytes 388
  149.1 3.5 %copy-start.2 = (bf16[72,4,2,128]{3,2,1,0:T(2,128)(2,1)S(1)}, bf16[72,4,2,128]{3,2,1,0:T(2,128)(2,1)}, u32[]{:S(2)}) copy-start(bf16[72,4,2,128]{3,2,1,0:T(2,128)(2,1)} %param.23) | copy-start | bytes 442372
  172.9 14.2 %copy-start.1 = (bf16[8,2,1,64,128]{4,3,2,1,0:T(8,128)(2,1)S(1)}, bf16[8,2,1,64,128]{4,3,2,1,0:T(8,128)(2,1)}, u32[]{:S(2)}) copy-start(bf16[8,2,1,64,128]{4,3,2,1,0:T(8,128)(2,1)} %get-tuple-element.10) | copy-start | bytes 786436
  174.8 19.0 %all-to-all-start.3 = ((bf16[64,4,512]{2,1,0:T(4,128)(2,1)}), bf16[64,4,512]{2,1,0:T(4,128)(2,1)}, u32[]{:S(2)}, u32[]{:S(2)}) async-start(bf16[64,4,512]{2,1,0:T(4,128)(2,1)} %copy.173), calls=%async_computation.3 | async-start | bytes 524288 | tf_op jit(solution)/shard_map/all_to_all | solution.py:94
  200.0 19.6 %all-to-all-start.4 = ((f32[64,1,16]{2,1,0:T(1,128)}), f32[64,1,16]{2,1,0:T(1,128)S(1)}, u32[]{:S(2)}, u32[]{:S(2)}) async-start(f32[64,1,16]{2,1,0:T(1,128)} %bitcast.18), calls=%async_computation.4 | async-start | bytes 65536 | tf_op jit(solution)/shard_map/all_to_all | solution.py:116
  213.1 25.2 %copy-start.4 = (bf16[72,4,4,4]{3,2,1,0:T(4,128)(2,1)S(1)}, bf16[72,4,4,4]{3,2,1,0:T(4,128)(2,1)}, u32[]{:S(2)}) copy-start(bf16[72,4,4,4]{3,2,1,0:T(4,128)(2,1)} %copy.196) | copy-start | bytes 27652
  213.1 25.2 %copy-start.5 = (f32[72,4,4]{2,1,0:T(4,128)S(1)}, f32[72,4,4]{2,1,0:T(4,128)}, u32[]{:S(2)}) copy-start(f32[72,4,4]{2,1,0:T(4,128)} %copy.205) | copy-start | bytes 13828
  219.6 17.9 %all-to-all-start.5 = ((bf16[64,2,1024]{2,1,0:T(2,128)(2,1)}), bf16[64,2,1024]{2,1,0:T(2,128)(2,1)S(1)}, u32[]{:S(2)}, u32[]{:S(2)}) async-start(bf16[64,2,1024]{2,1,0:T(2,128)(2,1)} %reshape.422), calls=%async_computation.5 | async-start | bytes 524288 | tf_op jit(solution)/shard_map/all_to_all | solution.py:115
Sparse Core Ops, SparseCore 0:
  61.2 68.6 all-reduce.1

commit v2 on v0

v2 whole, which is shorter than its diff:
```python
import jax
import jax.numpy as jnp
from jax import lax
from jax.experimental import pallas as pl
from jax.experimental.pallas import tpu as pltpu
from jax.sharding import PartitionSpec as P

HEAD_WIDTH = 128
SCALE = HEAD_WIDTH ** (-0.5)
MESH = pl.DeviceIdType.MESH
PER_OWNER = 2
CORES = 2
Z_CHIPS = 8
CHUNK = 16


def kernel(
    page0_ref,
    page1_ref,
    length_ref,
    own_table_ref,
    own_length_ref,
    request_ref,
    store_row_ref,
    tokens_ref,
    shrink_hbm,
    expand_hbm,
    base_hbm,
    fresh_hbm,
    pages_hbm,
    own_pages_hbm,
    out_ref,
    shrink_ref,
    expand_ref,
    base_ref,
    fresh_ref,
    pages_ref,
    own_pages_ref,
    gather_ref,
    x_send,
    x_recv,
    pick_send,
    pick_recv,
    part_send,
    part_recv,
    delta_send,
    delta_recv,
    fresh_recv,
    query_ref,
    query_recv,
    mixed_send,
    own_mixed,
    score_ref,
    weight_ref,
    mix_ref,
    load_sem,
    x_sem,
    pick_sem,
    part_sem,
    query_sem,
    one_sem,
    send_sem,
):
    groups = x_send.shape[0]
    peers = lax.axis_size("tp")
    slots = base_ref.shape[0]
    resident = own_length_ref.shape[0]
    steps = 4
    block = PER_OWNER * steps
    chunk = min(CHUNK, groups)
    chunks = groups // chunk
    rank = 64
    me = lax.axis_index("pool")
    row = lax.axis_index("tp")
    z_chips = min(Z_CHIPS, groups // CORES)
    x_chips = groups // (z_chips * CORES)
    my_x, my_z, my_core = me // (z_chips * CORES), (me // CORES) % z_chips, me % CORES

    def partner(k, sign):
        at_x, at, at_core = k // (z_chips * CORES), (k // CORES) % z_chips, k % CORES
        odd = at % 2
        at_z = odd * ((at + 1) // 2) + (1 - odd) * ((z_chips - at // 2) % z_chips)
        if sign < 0:
            at_x, at_z, at_core = x_chips - at_x, z_chips - at_z, CORES - at_core
        to_x = lax.rem(my_x + at_x, x_chips)
        to_z = lax.rem(my_z + at_z, z_chips)
        to_core = lax.rem(my_core + at_core, CORES)
        return (to_x * z_chips + to_z) * CORES + to_core

    barrier = pltpu.get_barrier_semaphore()

    @pl.loop(1, groups)
    def _(k):
        pl.semaphore_signal(
            barrier, inc=1, device_id={"pool": partner(k, 1)}, device_id_type=MESH
        )

    @pl.loop(1, peers)
    def _(j):
        pl.semaphore_signal(
            barrier, inc=1, device_id={"tp": lax.rem(row + j, peers)}, device_id_type=MESH
        )

    loads = [
        pltpu.make_async_copy(source, target, load_sem.at[n])
        for n, (source, target) in enumerate(
            [
                (shrink_hbm, shrink_ref),
                (expand_hbm, expand_ref),
                (base_hbm, base_ref),
                (fresh_hbm, fresh_ref),
                (pages_hbm, pages_ref),
                (own_pages_hbm, own_pages_ref),
            ]
        )
    ]
    for load in loads:
        load.start()

    stored = shrink_ref.shape[0] // rank
    adapters = store_row_ref.shape[1]
    store_row = store_row_ref[...]
    request = request_ref[...]
    half = lax.broadcasted_iota(jnp.int32, (8, adapters), 0)
    parts = jnp.where(half == 0, store_row // stored, store_row % stored)
    named = lax.broadcasted_iota(jnp.int32, (adapters, slots), 0) == request
    found = jnp.dot(
        parts.astype(jnp.float32).astype(jnp.bfloat16),
        jnp.where(named, 1.0, 0.0).astype(jnp.bfloat16),
        preferred_element_type=jnp.float32,
    )
    holder, within = found[0:1], found[1:2]
    slot_row = lax.broadcasted_iota(jnp.int32, (slots, slots), 0)
    slot_col = lax.broadcasted_iota(jnp.int32, (slots, slots), 1)
    holder_col = jnp.sum(
        jnp.where(slot_row == slot_col, holder, 0.0), axis=1, keepdims=True
    )
    earlier = (holder_col == holder) & (slot_row < slot_col)
    place = holder * PER_OWNER + jnp.sum(
        jnp.where(earlier, 1.0, 0.0), axis=0, keepdims=True
    )

    holder_ids = lax.broadcasted_iota(jnp.int32, (groups, slots), 0).astype(jnp.float32)
    wanted = jnp.max(jnp.where(holder_ids == holder, within, 0.0), axis=1, keepdims=True)
    pick_send[...] = jnp.broadcast_to(wanted, (groups, HEAD_WIDTH)).reshape(
        groups, 1, HEAD_WIDTH
    )

    wide = slots * steps
    widen = lax.broadcasted_iota(
        jnp.int32, (slots, wide), 1
    ) // steps == lax.broadcasted_iota(jnp.int32, (slots, wide), 0)
    place_wide = jnp.dot(
        jnp.broadcast_to(place, (8, slots)).astype(jnp.bfloat16),
        jnp.where(widen, 1.0, 0.0).astype(jnp.bfloat16),
        preferred_element_type=jnp.float32,
    )[0:1]
    step_of = lax.broadcasted_iota(jnp.int32, (1, wide), 1) % steps
    place_wide = place_wide * steps + step_of.astype(jnp.float32)
    row_ids = lax.broadcasted_iota(jnp.int32, (groups * block, wide), 0).astype(jnp.float32)
    dispatch = jnp.where(row_ids == place_wide, 1.0, 0.0).astype(jnp.bfloat16)
    outgoing = jnp.dot(dispatch, tokens_ref[...], preferred_element_type=jnp.float32)
    x_send[...] = outgoing.reshape(x_send.shape).astype(jnp.bfloat16)

    pl.semaphore_wait(barrier, groups - 1 + peers - 1)

    @pl.loop(1, groups)
    def _(k):
        to = partner(k, -1)
        pltpu.make_async_remote_copy(
            x_send.at[to],
            x_recv.at[k],
            send_sem.at[0],
            x_sem.at[k // chunk],
            device_id={"pool": to},
            device_id_type=MESH,
        ).start()
        pltpu.make_async_remote_copy(
            pick_send.at[to],
            pick_recv.at[k],
            send_sem.at[1],
            pick_sem.at[k // chunk],
            device_id={"pool": to},
            device_id_type=MESH,
        ).start()

    pltpu.make_async_copy(x_send.at[me], x_recv.at[0], x_sem.at[0]).start()
    pltpu.make_async_copy(pick_send.at[me], pick_recv.at[0], pick_sem.at[0]).start()

    span = slots * block
    line = lax.broadcasted_iota(jnp.int32, (span, slots), 0)
    own_line = line // block == lax.broadcasted_iota(jnp.int32, (span, slots), 1)
    holder_line = jnp.sum(jnp.where(own_line, holder, 0.0), axis=1, keepdims=True)
    place_line = jnp.sum(jnp.where(own_line, place, 0.0), axis=1, keepdims=True)
    inner = lax.broadcasted_iota(jnp.int32, (span, 1), 0) % block
    inner = (inner // steps) * block + inner % steps
    source = (
        holder_line * (2 * block)
        + (place_line - holder_line * PER_OWNER) * steps
        + inner.astype(jnp.float32)
    )
    column = lax.broadcasted_iota(jnp.int32, (span, groups * 2 * block), 1)
    gather_ref[...] = jnp.where(column.astype(jnp.float32) == source, 1.0, 0.0).astype(
        jnp.bfloat16
    )

    loads[0].wait()
    loads[1].wait()
    lanes = HEAD_WIDTH // rank
    rows = chunk * block
    tiles = stored // lanes
    lane = lax.broadcasted_iota(jnp.int32, (rows, HEAD_WIDTH), 1)
    lane_half = (lane // rank).astype(jnp.float32)
    low_lane = lax.broadcasted_iota(jnp.int32, (rows // 2, HEAD_WIDTH), 1) < rank

    def wait_for(ref, sem):
        pltpu.make_async_copy(ref, ref, sem).wait()

    def picked(c):
        pick = pick_recv[pl.ds(c * chunk, chunk)]
        return jnp.broadcast_to(pick, (chunk, block, HEAD_WIDTH)).reshape(rows, HEAD_WIDTH)

    def shrink_chunk(c):
        here = pl.ds(c * chunk, chunk)
        wait_for(x_recv.at[here], x_sem.at[c])
        wait_for(pick_recv.at[here], pick_sem.at[c])
        x = x_recv[here].reshape(rows, x_recv.shape[2])
        every = lax.dot_general(
            x, shrink_ref[...], (((1,), (1,)), ((), ())), preferred_element_type=jnp.float32
        )
        pick = picked(c)
        low = jnp.zeros((rows, HEAD_WIDTH), jnp.float32)
        for tile in range(tiles):
            part = every[:, tile * HEAD_WIDTH : (tile + 1) * HEAD_WIDTH]
            low += jnp.where(pick == lane_half + tile * lanes, part, 0.0)
        low += pltpu.roll(low, rank, 1)
        part_send[c] = jnp.where(low_lane, low[: rows // 2], low[rows // 2 :]).astype(
            jnp.bfloat16
        )
        pltpu.make_async_copy(
            part_send.at[c], part_recv.at[c, row], part_sem.at[c]
        ).start()

        @pl.loop(1, peers)
        def _(j):
            pltpu.make_async_remote_copy(
                part_send.at[c],
                part_recv.at[c, row],
                send_sem.at[2],
                part_sem.at[c],
                device_id={"tp": lax.rem(row + j, peers)},
                device_id_type=MESH,
            ).start()

    def expand_chunk(c):
        wait_for(part_recv.at[c], part_sem.at[c])
        total = jnp.sum(part_recv[c].astype(jnp.float32), axis=0)
        total = total.astype(jnp.bfloat16).astype(jnp.float32)
        turned = pltpu.roll(total, rank, 1)
        low = jnp.concatenate(
            [jnp.where(low_lane, total, turned), jnp.where(low_lane, turned, total)], 0
        )
        pick = picked(c)
        spread = jnp.concatenate(
            [jnp.where(pick == lane_half + tile * lanes, low, 0.0) for tile in range(tiles)], 1
        ).astype(jnp.bfloat16)
        delta = jnp.dot(spread, expand_ref[...], preferred_element_type=jnp.float32)
        here = pl.ds(c * chunk, chunk)
        for head in range(4):
            piece = delta[:, head * HEAD_WIDTH : (head + 1) * HEAD_WIDTH]
            delta_send[here, head * block : (head + 1) * block, :] = piece.reshape(
                chunk, block, HEAD_WIDTH
            ).astype(jnp.bfloat16)

        @pl.loop(c * chunk, (c + 1) * chunk)
        def _(k):
            @pl.when(k > 0)
            def _():
                pltpu.make_async_remote_copy(
                    delta_send.at[k],
                    delta_recv.at[me],
                    send_sem.at[3],
                    one_sem.at[0],
                    device_id={"pool": partner(k, 1)},
                    device_id_type=MESH,
                ).start()

    shrink_chunk(0)

    @pl.loop(1, chunks)
    def _(c):
        shrink_chunk(c)
        expand_chunk(c - 1)

    expand_chunk(chunks - 1)
    pltpu.make_async_copy(delta_send.at[0], delta_recv.at[me], one_sem.at[0]).start()

    loads[3].wait()

    @pl.loop(1, groups)
    def _(k):
        to = partner(k, -1)
        pltpu.make_async_remote_copy(
            fresh_ref.at[resident + to],
            fresh_recv.at[k],
            send_sem.at[4],
            one_sem.at[1],
            device_id={"pool": to},
            device_id_type=MESH,
        ).start()

    pltpu.make_async_copy(fresh_ref.at[resident + me], fresh_recv.at[0], one_sem.at[1]).start()
    loads[2].wait()
    loads[4].wait()
    loads[5].wait()

    wait_for(delta_recv, one_sem.at[0])
    for pair in range(2):
        here = slice(pair * 2 * block, (pair + 1) * 2 * block)
        delta = jnp.dot(
            gather_ref[...],
            delta_recv[:, here, :].reshape(groups * 2 * block, HEAD_WIDTH),
            preferred_element_type=jnp.float32,
        ).reshape(slots, block, HEAD_WIDTH)
        mine = slice(pair * block, (pair + 1) * block)
        query_ref[:, mine, :] = (base_ref[:, mine, :].astype(jnp.float32) + delta).astype(
            jnp.bfloat16
        )

    @pl.loop(1, groups)
    def _(k):
        to = partner(k, -1)
        pltpu.make_async_remote_copy(
            query_ref.at[resident + to],
            query_recv.at[k],
            send_sem.at[5],
            query_sem.at[k // chunk],
            device_id={"pool": to},
            device_id_type=MESH,
        ).start()

    pltpu.make_async_copy(
        query_ref.at[resident + me], query_recv.at[0], query_sem.at[0]
    ).start()

    def attend(number, queries, fresh, slot_pages, slot_length, pool_ref):
        lines = number * 16
        flat = queries.reshape(lines, HEAD_WIDTH)
        new = fresh.reshape(-1, HEAD_WIDTH)
        new_scores = (
            lax.dot_general(
                flat, new, (((1,), (1,)), ((), ())), preferred_element_type=jnp.float32
            )
            * SCALE
        )
        at = lax.broadcasted_iota(jnp.int32, new_scores.shape, 0)
        key = lax.broadcasted_iota(jnp.int32, new_scores.shape, 1)
        seen = (at // 16 == key // 8) & ((key % 8) // 2 <= at % steps) & (key % 2 == 0)
        new_scores = jnp.where(seen, new_scores, -jnp.inf)
        position = lax.broadcasted_iota(jnp.int32, (16, HEAD_WIDTH), 1)
        for m in range(number):
            first, second = slot_pages(m)
            keys = jnp.concatenate([pool_ref[first, 0], pool_ref[second, 0]], 0)
            scores = lax.dot_general(
                queries[m], keys, (((1,), (1,)), ((), ())), preferred_element_type=jnp.float32
            )
            score_ref[m * 16 : (m + 1) * 16, :] = jnp.where(
                position < slot_length(m), scores * SCALE, -jnp.inf
            )
        scores = score_ref[:lines, :]
        highest = jnp.maximum(
            jnp.max(scores, axis=1, keepdims=True), jnp.max(new_scores, axis=1, keepdims=True)
        )
        weights = jnp.exp(scores - highest)
        new_weights = jnp.exp(new_scores - highest)
        total = jnp.sum(weights, axis=1, keepdims=True) + jnp.sum(
            new_weights, axis=1, keepdims=True
        )
        weight_ref[:lines, :] = weights.astype(jnp.bfloat16)
        for m in range(number):
            first, second = slot_pages(m)
            values = jnp.concatenate([pool_ref[first, 1], pool_ref[second, 1]], 0)
            mixed = jnp.dot(
                weight_ref[m * 16 : (m + 1) * 16, :], values, preferred_element_type=jnp.float32
            )
            mix_ref[m * 16 : (m + 1) * 16, :] = jnp.where(slot_length(m) > 0, mixed, 0.0)
        moved = pltpu.roll(new_weights, 1, 1).astype(jnp.bfloat16)
        new_mixed = jnp.dot(moved, new, preferred_element_type=jnp.float32)
        return (mix_ref[:lines, :] + new_mixed) / total

    own = attend(
        resident,
        query_ref[:resident],
        fresh_ref[:chunk],
        lambda m: (own_table_ref[m, 0], own_table_ref[m, 1]),
        lambda m: own_length_ref[m],
        own_pages_ref,
    )
    own_mixed[...] = own.reshape(own_mixed.shape).astype(jnp.bfloat16)
    own_copy = pltpu.make_async_copy(own_mixed, out_ref.at[pl.ds(0, resident)], one_sem.at[3])
    own_copy.start()

    wait_for(fresh_recv, one_sem.at[1])

    @pl.loop(0, chunks)
    def _(c):
        here = pl.ds(c * chunk, chunk)
        wait_for(query_recv.at[here], query_sem.at[c])
        at = [partner(c * chunk + m, 1) for m in range(chunk)]
        mixed = attend(
            chunk,
            query_recv[here],
            fresh_recv[here],
            lambda m: (page0_ref[at[m]], page1_ref[at[m]]),
            lambda m: length_ref[at[m]],
            pages_ref,
        ).reshape(chunk, 16, HEAD_WIDTH)
        for m in range(chunk):
            mixed_send[c * chunk + m] = jnp.where(length_ref[at[m]] > 0, mixed[m], 0.0).astype(
                jnp.bfloat16
            )

        @pl.loop(c * chunk, (c + 1) * chunk)
        def _(k):
            @pl.when(k > 0)
            def _():
                pltpu.make_async_remote_copy(
                    mixed_send.at[k],
                    out_ref.at[resident + me],
                    send_sem.at[6],
                    one_sem.at[2],
                    device_id={"pool": partner(k, 1)},
                    device_id_type=MESH,
                ).start()

    pltpu.make_async_copy(
        mixed_send.at[0], out_ref.at[resident + me], one_sem.at[2]
    ).start()

    others = pl.ds(0, groups - 1)
    wait_for(x_send.at[others], send_sem.at[0])
    wait_for(pick_send.at[others], send_sem.at[1])
    wait_for(part_recv.at[:, pl.ds(0, peers - 1)], send_sem.at[2])
    wait_for(delta_send.at[others], send_sem.at[3])
    wait_for(fresh_recv.at[others], send_sem.at[4])
    wait_for(query_recv.at[others], send_sem.at[5])
    wait_for(mixed_send.at[others], send_sem.at[6])
    own_copy.wait()
    wait_for(mixed_send, one_sem.at[2])


def body(
    prefill_page_pool,
    prefill_page_table,
    prefill_length,
    prefill_target_group,
    resident_page_pool,
    resident_page_table,
    resident_length,
    tokens,
    base_query_projection,
    fresh_key_value,
    request_adapter,
    adapter_store_row,
    shrink_weight,
    expand_weight,
):
    groups = lax.axis_size("pool")
    peers = lax.axis_size("tp")
    slots, steps, width = tokens.shape
    stored, rank, _ = shrink_weight.shape
    out_width = expand_weight.shape[2]
    heads = out_width // HEAD_WIDTH
    resident = resident_length.shape[0]
    block = PER_OWNER * steps
    lines = heads * steps
    chunk = min(CHUNK, groups)
    chunks = groups // chunk

    group_ids = jnp.arange(groups, dtype=jnp.int32)
    meant = prefill_target_group[:, None] == group_ids[None, :]
    page0 = jnp.sum(jnp.where(meant, prefill_page_table[:, 0:1], 0), axis=0)
    page1 = jnp.sum(jnp.where(meant, prefill_page_table[:, 1:2], 0), axis=0)
    length = jnp.sum(jnp.where(meant, prefill_length[:, None], 0), axis=0)
    base = (
        base_query_projection.reshape(slots, steps, heads, HEAD_WIDTH)
        .transpose(0, 2, 1, 3)
        .reshape(slots, lines, HEAD_WIDTH)
    )
    operands = [
        page0,
        page1,
        length,
        resident_page_table,
        resident_length,
        request_adapter.reshape(1, slots),
        adapter_store_row.reshape(1, -1),
        tokens.reshape(slots * steps, width),
        shrink_weight.reshape(stored * rank, width),
        expand_weight.reshape(stored * rank, out_width),
        base,
        fresh_key_value.reshape(slots, 2 * steps, HEAD_WIDTH),
        prefill_page_pool,
        resident_page_pool,
    ]
    smem = pl.BlockSpec(memory_space=pltpu.SMEM)
    vmem = pl.BlockSpec(memory_space=pltpu.VMEM)
    hbm = pl.BlockSpec(memory_space=pl.ANY)
    half = jnp.bfloat16
    dma = pltpu.SemaphoreType.DMA
    out = pl.pallas_call(
        kernel,
        out_shape=jax.ShapeDtypeStruct((slots, lines, HEAD_WIDTH), half),
        in_specs=[smem] * 5 + [vmem] * 3 + [hbm] * 6,
        out_specs=hbm,
        scratch_shapes=[
            pltpu.VMEM(operand.shape, half) for operand in operands[8:]
        ]
        + [
            pltpu.VMEM((slots * block, groups * 2 * block), half),
            pltpu.VMEM((groups, block, width), half),
            pltpu.VMEM((groups, block, width), half),
            pltpu.VMEM((groups, 1, HEAD_WIDTH), jnp.float32),
            pltpu.VMEM((groups, 1, HEAD_WIDTH), jnp.float32),
            pltpu.VMEM((chunks, chunk * block // 2, HEAD_WIDTH), half),
            pltpu.VMEM((chunks, peers, chunk * block // 2, HEAD_WIDTH), half),
            pltpu.VMEM((groups, heads * block, HEAD_WIDTH), half),
            pltpu.VMEM((groups, heads * block, HEAD_WIDTH), half),
            pltpu.VMEM((groups, 2 * steps, HEAD_WIDTH), half),
            pltpu.VMEM((slots, lines, HEAD_WIDTH), half),
            pltpu.VMEM((groups, lines, HEAD_WIDTH), half),
            pltpu.VMEM((groups, lines, HEAD_WIDTH), half),
            pltpu.VMEM((resident, lines, HEAD_WIDTH), half),
            pltpu.VMEM((chunk * lines, HEAD_WIDTH), jnp.float32),
            pltpu.VMEM((chunk * lines, HEAD_WIDTH), half),
            pltpu.VMEM((chunk * lines, HEAD_WIDTH), jnp.float32),
            dma((6,)),
            dma((chunks,)),
            dma((chunks,)),
            dma((chunks,)),
            dma((chunks,)),
            dma((4,)),
            dma((7,)),
        ],
        compiler_params=pltpu.CompilerParams(
            collective_id=0, has_side_effects=True, vmem_limit_bytes=48 * 1024 * 1024
        ),
    )(*operands)
    return (
        out.reshape(slots, heads, steps, HEAD_WIDTH)
        .transpose(0, 2, 1, 3)
        .reshape(slots, steps, out_width)
    )


def solution(mesh):
    return jax.shard_map(
        body,
        mesh=mesh,
        in_specs=(
            P("pool", None, None, "tp"),
            P("pool", None),
            P("pool"),
            P("pool"),
            P("pool", None, None, "tp"),
            P("pool", None),
            P("pool"),
            P("pool", None, "tp"),
            P("pool", None, "tp"),
            P("pool", None, None, "tp"),
            P("pool"),
            P(),
            P("pool", None, "tp"),
            P("pool", None, "tp"),
        ),
        out_specs=P("pool", None, "tp"),
        check_vma=False,
    )
```

time: 387 us -> 86.8 us (0.22)
  waiting for transfers between devices: 233 us -> 0 us
  Pallas kernels: 0 us -> 73.7 us
  starting transfers between devices: 42.2 us -> 0 us
  other arithmetic: 30.3 us -> 0.77 us
  blocking collectives: 27.3 us -> 0 us
  local copies, waits for them, and re-layouts: 36.6 us -> 11.9 us
  matrix products: 16.1 us -> 0 us
    all_to_all x5 -> x0, waiting for transfers between devices: 233 us -> none  [the longest x1 111 us: body(): lax.all_to_all(shrink_factor[:, None], 'pool', split_axis=0, concat_axis=...]
    pallas_call x0 -> x1, Pallas kernels: none -> 73.7 us  [body(): pl.pallas_call(kernel, out_shape=jax.ShapeDtypeStruct((slots, lines, HEAD...]
    all_to_all x5 -> x0, starting transfers between devices: 42.2 us -> none  [the longest x1 14.8 us: body(): lax.all_to_all(wanted[:, None], 'pool', split_axis=0, concat_axis=0, tile...]
    psum x1 -> x0, blocking collectives: 27.3 us -> none  [body(): rank_product = lax.psum(own_part.astype(jnp.bfloat16), 'tp')]
    dot_general x4 -> x0, matrix products: 16.1 us -> none  [the longest x1 6.75 us: body(): lax.dot_general(tokens.reshape(total_slot_count * decode_step_count, -1),...]
    select_n x9 -> x0, other arithmetic: 14.3 us -> none  [the longest x2 5.39 us: body(): shrink_factor = jnp.where(present_mask, shrink_weight[clipped_length], 0)]
    unnamed x26 -> x20, local copies, waits for them, and re-layouts: 0.16 us -> 10.1 us
    gather x4 -> x0, local copies, waits for them, and re-layouts: 9.17 us -> none  [the longest x1 3.53 us: body(): shrink_factor = jnp.where(present_mask, shrink_weight[clipped_length], 0)]
  transfers between devices with their start and end apart: 5 -> 0, of which waited for: 4 -> 0; matrix products, arithmetic and copies ran while one was open for 18% -> 0% of each run, Pallas kernels for 0% -> 0%
where the time goes in v2:
time: 86.8 us; the launch traced here: 86.4 us
  Pallas kernels  73.7 us (85%)
  local copies, waits for them, and re-layouts  11.9 us (14%)
    pallas_call x1, Pallas kernels, body(): pl.pallas_call(kernel, out_shape=jax.ShapeDtypeStruct((slots, lines, HEAD...  73.7 us
    unnamed x20, local copies, waits for them, and re-layouts  10.1 us

profile of v2, /device:TPU:1, one launch (start us, length us, event | category | flops | bytes accessed | tf_op | source)
XLA Modules:
  0.0 86.4 jit_solution(12340304841370578501)
XLA Ops:
  0.0 0.8 slice_bitcast_fusion.1
  0.8 0.8 select_reduce_fusion
  1.5 0.8 copy.19.own_table_ref
  2.3 1.1 %reshape.34.tokens_ref = bf16[288,640]{1,0:T(8,128)(2,1)S(1)} reshape(bf16[72,4,640]{2,1,0:T(4,128)(2,1)} %param.21) | data formatting | bytes 737280 | tf_op jit(solution)/shard_map/reshape | solution.py:498
  3.4 0.0 copy-start
  3.4 1.6 %copy-done = bf16[64,2,64,128]{3,2,1,0:T(8,128)(2,1)S(1)} copy-done((bf16[64,2,64,128]{3,2,1,0:T(8,128)(2,1)S(1)}, bf16[64,2,64,128]{3,2,1,0:T(8,128)(2,1)}, u32[]{:S(2)}) %copy-start) | copy-done | bytes 2097176
  5.0 0.0 copy-start.1
  5.0 1.1 %copy-done.1 = bf16[8,64,640]{2,1,0:T(8,128)(2,1)S(1)} copy-done((bf16[8,64,640]{2,1,0:T(8,128)(2,1)S(1)}, bf16[8,64,640]{2,1,0:T(8,128)(2,1)}, u32[]{:S(2)}) %copy-start.1) | copy-done | bytes 655384
  6.0 0.0 copy-start.2
  6.0 1.0 %copy-done.2 = bf16[8,64,512]{2,1,0:T(8,128)(2,1)S(1)} copy-done((bf16[8,64,512]{2,1,0:T(8,128)(2,1)S(1)}, bf16[8,64,512]{2,1,0:T(8,128)(2,1)}, u32[]{:S(2)}) %copy-start.2) | copy-done | bytes 524312
  7.1 0.0 copy-start.3
  7.1 1.0 %copy-done.3 = bf16[16,2,64,128]{3,2,1,0:T(8,128)(2,1)S(1)} copy-done((bf16[16,2,64,128]{3,2,1,0:T(8,128)(2,1)S(1)}, bf16[16,2,64,128]{3,2,1,0:T(8,128)(2,1)}, u32[]{:S(2)}) %copy-start.3) | copy-done | bytes 524312
  8.1 0.0 copy-start.4
  8.1 1.0 %copy-done.4 = bf16[72,4,512]{2,1,0:T(4,128)(2,1)S(1)} copy-done((bf16[72,4,512]{2,1,0:T(4,128)(2,1)S(1)}, bf16[72,4,512]{2,1,0:T(4,128)(2,1)}, u32[]{:S(2)}) %copy-start.4) | copy-done | bytes 294936
  9.1 0.0 copy-start.5
  9.1 0.9 %copy-done.5 = bf16[72,4,2,128]{3,2,1,0:T(2,128)(2,1)S(1)} copy-done((bf16[72,4,2,128]{3,2,1,0:T(2,128)(2,1)S(1)}, bf16[72,4,2,128]{3,2,1,0:T(2,128)(2,1)}, u32[]{:S(2)}) %copy-start.5) | copy-done | bytes 147480
  10.0 0.0 copy-start.6
  10.0 0.7 copy-done.6
  10.7 0.0 copy-start.7
  10.7 0.7 copy-done.7
  11.3 0.0 copy-start.8
  11.3 0.7 copy-done.8
  12.0 73.7 %shard_map.136 = bf16[72,16,128]{2,1,0:T(8,128)(2,1)S(1)} custom-call(s32[64]{0:T(128)S(1)} %get-tuple-element.7.page0_ref, s32[64]{0:T(128)S(1)} %get-tuple-element.6.page1_ref, s32[64]{0:T(128)S(1)} %get-tuple-element.5.length_ref, s32[8,2]{1,0:T(8,128)S(1)} %copy.19.own_table_ref, s32[8]{0:T(128)S(1)} %copy-done.7, s32[1,72]{1,0:T(1,128)S(1)} %bitcast.25, ...), custom_call_target="tpu_custom_call" | custom-call | tf_op jit(solution)/shard_map/pallas_call | solution.py:511
  85.7 0.7 copy.22
Async XLA Ops:
  3.4 1.6 %copy-start = (bf16[64,2,64,128]{3,2,1,0:T(8,128)(2,1)S(1)}, bf16[64,2,64,128]{3,2,1,0:T(8,128)(2,1)}, u32[]{:S(2)}) copy-start(bf16[64,2,64,128]{3,2,1,0:T(8,128)(2,1)} %pages_hbm.1) | copy-start | bytes 6291460
  5.0 1.1 %copy-start.1 = (bf16[8,64,640]{2,1,0:T(8,128)(2,1)S(1)}, bf16[8,64,640]{2,1,0:T(8,128)(2,1)}, u32[]{:S(2)}) copy-start(bf16[8,64,640]{2,1,0:T(8,128)(2,1)} %param.26) | copy-start | bytes 1966084
  6.0 1.0 %copy-start.2 = (bf16[8,64,512]{2,1,0:T(8,128)(2,1)S(1)}, bf16[8,64,512]{2,1,0:T(8,128)(2,1)}, u32[]{:S(2)}) copy-start(bf16[8,64,512]{2,1,0:T(8,128)(2,1)} %param.27) | copy-start | bytes 1572868
  7.1 1.0 %copy-start.3 = (bf16[16,2,64,128]{3,2,1,0:T(8,128)(2,1)S(1)}, bf16[16,2,64,128]{3,2,1,0:T(8,128)(2,1)}, u32[]{:S(2)}) copy-start(bf16[16,2,64,128]{3,2,1,0:T(8,128)(2,1)} %own_pages_hbm.1) | copy-start | bytes 1572868
  8.1 1.0 %copy-start.4 = (bf16[72,4,512]{2,1,0:T(4,128)(2,1)S(1)}, bf16[72,4,512]{2,1,0:T(4,128)(2,1)}, u32[]{:S(2)}) copy-start(bf16[72,4,512]{2,1,0:T(4,128)(2,1)} %param.22) | copy-start | bytes 884740
  9.1 0.9 %copy-start.5 = (bf16[72,4,2,128]{3,2,1,0:T(2,128)(2,1)S(1)}, bf16[72,4,2,128]{3,2,1,0:T(2,128)(2,1)}, u32[]{:S(2)}) copy-start(bf16[72,4,2,128]{3,2,1,0:T(2,128)(2,1)} %param.23) | copy-start | bytes 442372
  10.0 0.7 copy-start.6
  10.7 0.7 copy-start.7
  11.3 0.7 copy-start.8

commit v3 on v2

--- a/solution.py
+++ b/solution.py
@@ -1,3 +1,5 @@
+import functools
+
 import jax
 import jax.numpy as jnp
 from jax import lax
@@ -11,18 +13,18 @@
 PER_OWNER = 2
 CORES = 2
 Z_CHIPS = 8
-CHUNK = 16
+FRESH_SLOTS = HEAD_WIDTH // 8
 
 
 def kernel(
-    page0_ref,
-    page1_ref,
-    length_ref,
-    own_table_ref,
-    own_length_ref,
-    request_ref,
-    store_row_ref,
-    tokens_ref,
+    target_hbm,
+    length_hbm,
+    table_hbm,
+    own_length_hbm,
+    own_table_hbm,
+    request_hbm,
+    store_row_hbm,
+    tokens_hbm,
     shrink_hbm,
     expand_hbm,
     base_hbm,
@@ -30,12 +32,22 @@
     pages_hbm,
     own_pages_hbm,
     out_ref,
+    target_ref,
+    length_ref,
+    table_ref,
+    own_length_ref,
+    own_table_ref,
+    request_ref,
+    store_row_ref,
+    tokens_ref,
     shrink_ref,
     expand_ref,
     base_ref,
     fresh_ref,
     pages_ref,
     own_pages_ref,
+    plan_line,
+    plan_ref,
     gather_ref,
     x_send,
     x_recv,
@@ -67,44 +79,61 @@
     resident = own_length_ref.shape[0]
     steps = 4
     block = PER_OWNER * steps
-    chunk = min(CHUNK, groups)
-    chunks = groups // chunk
     rank = 64
     me = lax.axis_index("pool")
     row = lax.axis_index("tp")
-    z_chips = min(Z_CHIPS, groups // CORES)
+    z_chips = Z_CHIPS
     x_chips = groups // (z_chips * CORES)
     my_x, my_z, my_core = me // (z_chips * CORES), (me // CORES) % z_chips, me % CORES
 
-    def partner(k, sign):
-        at_x, at, at_core = k // (z_chips * CORES), (k // CORES) % z_chips, k % CORES
-        odd = at % 2
-        at_z = odd * ((at + 1) // 2) + (1 - odd) * ((z_chips - at // 2) % z_chips)
-        if sign < 0:
-            at_x, at_z, at_core = x_chips - at_x, z_chips - at_z, CORES - at_core
-        to_x = lax.rem(my_x + at_x, x_chips)
-        to_z = lax.rem(my_z + at_z, z_chips)
-        to_core = lax.rem(my_core + at_core, CORES)
-        return (to_x * z_chips + to_z) * CORES + to_core
-
-    barrier = pltpu.get_barrier_semaphore()
-
-    @pl.loop(1, groups)
-    def _(k):
-        pl.semaphore_signal(
-            barrier, inc=1, device_id={"pool": partner(k, 1)}, device_id_type=MESH
-        )
-
-    @pl.loop(1, peers)
-    def _(j):
-        pl.semaphore_signal(
-            barrier, inc=1, device_id={"tp": lax.rem(row + j, peers)}, device_id_type=MESH
-        )
+    chunk = 2 * x_chips * CORES
+    chunks = groups // chunk
+    turns = sorted(range(x_chips), key=lambda x: -min(x, x_chips - x))
+    last, self_m = chunks - 1, chunk - CORES
+    self_k = last * chunk + self_m
+    ahead = [lax.rem(my_x + x, x_chips) * (z_chips * CORES) for x in turns]
+    behind = [lax.rem(my_x + (x_chips - x), x_chips) * (z_chips * CORES) for x in turns]
+    cores = [my_core, 1 - my_core]
+
+    def partners(c, sign):
+        offsets = (z_chips // 2 + c, z_chips // 2 - 1 - c)
+        to_z = [
+            lax.rem(my_z + (z if sign > 0 else z_chips - z), z_chips) * CORES for z in offsets
+        ]
+        return [
+            to_x + z + core
+            for z in to_z
+            for to_x in (ahead if sign > 0 else behind)
+            for core in cores
+        ]
+
+    def to_chunk(c, sign, send):
+        for m, to in enumerate(partners(c, sign)):
+            if m == self_m:
+
+                @pl.when(c != last)
+                def _():
+                    send(c * chunk + m, to)
+            else:
+                send(c * chunk + m, to)
+
+    def to_all(sign, send):
+        @pl.loop(0, chunks)
+        def _(c):
+            to_chunk(c, sign, functools.partial(send, c))
 
     loads = [
         pltpu.make_async_copy(source, target, load_sem.at[n])
         for n, (source, target) in enumerate(
             [
+                (request_hbm, request_ref),
+                (store_row_hbm, store_row_ref),
+                (tokens_hbm, tokens_ref),
+                (target_hbm, target_ref),
+                (length_hbm, length_ref),
+                (table_hbm, table_ref),
+                (own_length_hbm, own_length_ref),
+                (own_table_hbm, own_table_ref),
                 (shrink_hbm, shrink_ref),
                 (expand_hbm, expand_ref),
                 (base_hbm, base_ref),
@@ -116,6 +145,22 @@
     ]
     for load in loads:
         load.start()
+
+    barrier = pltpu.get_barrier_semaphore()
+
+    def greet(c, k, to):
+        pl.semaphore_signal(barrier, inc=1, device_id={"pool": to}, device_id_type=MESH)
+
+    to_all(1, greet)
+
+    @pl.loop(1, peers)
+    def _(j):
+        pl.semaphore_signal(
+            barrier, inc=1, device_id={"tp": lax.rem(row + j, peers)}, device_id_type=MESH
+        )
+
+    for load in loads[:3]:
+        load.wait()
 
     stored = shrink_ref.shape[0] // rank
     adapters = store_row_ref.shape[1]
@@ -164,14 +209,12 @@
 
     pl.semaphore_wait(barrier, groups - 1 + peers - 1)
 
-    @pl.loop(1, groups)
-    def _(k):
-        to = partner(k, -1)
+    def send_tokens(c, k, to):
         pltpu.make_async_remote_copy(
             x_send.at[to],
             x_recv.at[k],
             send_sem.at[0],
-            x_sem.at[k // chunk],
+            x_sem.at[c],
             device_id={"pool": to},
             device_id_type=MESH,
         ).start()
@@ -179,13 +222,32 @@
             pick_send.at[to],
             pick_recv.at[k],
             send_sem.at[1],
-            pick_sem.at[k // chunk],
+            pick_sem.at[c],
             device_id={"pool": to},
             device_id_type=MESH,
         ).start()
 
-    pltpu.make_async_copy(x_send.at[me], x_recv.at[0], x_sem.at[0]).start()
-    pltpu.make_async_copy(pick_send.at[me], pick_recv.at[0], pick_sem.at[0]).start()
+    to_all(-1, send_tokens)
+
+    pltpu.make_async_copy(x_send.at[me], x_recv.at[self_k], x_sem.at[last]).start()
+    pltpu.make_async_copy(pick_send.at[me], pick_recv.at[self_k], pick_sem.at[last]).start()
+
+    for load in loads[3:8]:
+        load.wait()
+    group_lane = lax.broadcasted_iota(jnp.int32, (1, plan_line.shape[1]), 1)
+
+    def assign(j, lines):
+        hit = group_lane == target_ref[j]
+        found = (table_ref[0, j], table_ref[1, j], length_ref[j])
+        return tuple(jnp.where(hit, new, old) for new, old in zip(found, lines))
+
+    empty = jnp.zeros(group_lane.shape, jnp.int32)
+    lines = lax.fori_loop(0, target_ref.shape[0], assign, (empty, empty, empty))
+    plan_line[...] = jnp.zeros_like(plan_line)
+    for n in range(3):
+        plan_line[n : n + 1, :] = lines[n]
+    plan_copy = pltpu.make_async_copy(plan_line, plan_ref, load_sem.at[len(loads)])
+    plan_copy.start()
 
     span = slots * block
     line = lax.broadcasted_iota(jnp.int32, (span, slots), 0)
@@ -204,8 +266,9 @@
         jnp.bfloat16
     )
 
-    loads[0].wait()
-    loads[1].wait()
+    plan_copy.wait()
+    loads[8].wait()
+    loads[9].wait()
     lanes = HEAD_WIDTH // rank
     rows = chunk * block
     tiles = stored // lanes
@@ -272,18 +335,17 @@
                 chunk, block, HEAD_WIDTH
             ).astype(jnp.bfloat16)
 
-        @pl.loop(c * chunk, (c + 1) * chunk)
-        def _(k):
-            @pl.when(k > 0)
-            def _():
-                pltpu.make_async_remote_copy(
-                    delta_send.at[k],
-                    delta_recv.at[me],
-                    send_sem.at[3],
-                    one_sem.at[0],
-                    device_id={"pool": partner(k, 1)},
-                    device_id_type=MESH,
-                ).start()
+        def send_delta(k, to):
+            pltpu.make_async_remote_copy(
+                delta_send.at[k],
+                delta_recv.at[me],
+                send_sem.at[3],
+                one_sem.at[0],
+                device_id={"pool": to},
+                device_id_type=MESH,
+            ).start()
+
+        to_chunk(c, 1, send_delta)
 
     shrink_chunk(0)
 
@@ -293,13 +355,11 @@
         expand_chunk(c - 1)
 
     expand_chunk(chunks - 1)
-    pltpu.make_async_copy(delta_send.at[0], delta_recv.at[me], one_sem.at[0]).start()
-
-    loads[3].wait()
-
-    @pl.loop(1, groups)
-    def _(k):
-        to = partner(k, -1)
+    pltpu.make_async_copy(delta_send.at[self_k], delta_recv.at[me], one_sem.at[0]).start()
+
+    loads[11].wait()
+
+    def send_fresh(c, k, to):
         pltpu.make_async_remote_copy(
             fresh_ref.at[resident + to],
             fresh_recv.at[k],
@@ -309,10 +369,14 @@
             device_id_type=MESH,
         ).start()
 
-    pltpu.make_async_copy(fresh_ref.at[resident + me], fresh_recv.at[0], one_sem.at[1]).start()
-    loads[2].wait()
-    loads[4].wait()
-    loads[5].wait()
+    to_all(-1, send_fresh)
+
+    pltpu.make_async_copy(
+        fresh_ref.at[resident + me], fresh_recv.at[self_k], one_sem.at[1]
+    ).start()
+    loads[10].wait()
+    loads[12].wait()
+    loads[13].wait()
 
     wait_for(delta_recv, one_sem.at[0])
     for pair in range(2):
@@ -327,20 +391,20 @@
             jnp.bfloat16
         )
 
-    @pl.loop(1, groups)
-    def _(k):
-        to = partner(k, -1)
+    def send_query(c, k, to):
         pltpu.make_async_remote_copy(
             query_ref.at[resident + to],
             query_recv.at[k],
             send_sem.at[5],
-            query_sem.at[k // chunk],
+            query_sem.at[c],
             device_id={"pool": to},
             device_id_type=MESH,
         ).start()
 
+    to_all(-1, send_query)
+
     pltpu.make_async_copy(
-        query_ref.at[resident + me], query_recv.at[0], query_sem.at[0]
+        query_ref.at[resident + me], query_recv.at[self_k], query_sem.at[last]
     ).start()
 
     def attend(number, queries, fresh, slot_pages, slot_length, pool_ref):
@@ -391,8 +455,8 @@
     own = attend(
         resident,
         query_ref[:resident],
-        fresh_ref[:chunk],
-        lambda m: (own_table_ref[m, 0], own_table_ref[m, 1]),
+        fresh_ref[:FRESH_SLOTS],
+        lambda m: (own_table_ref[0, m], own_table_ref[1, m]),
         lambda m: own_length_ref[m],
         own_pages_ref,
     )
@@ -406,35 +470,34 @@
     def _(c):
         here = pl.ds(c * chunk, chunk)
         wait_for(query_recv.at[here], query_sem.at[c])
-        at = [partner(c * chunk + m, 1) for m in range(chunk)]
+        at = partners(c, 1)
         mixed = attend(
             chunk,
             query_recv[here],
             fresh_recv[here],
-            lambda m: (page0_ref[at[m]], page1_ref[at[m]]),
-            lambda m: length_ref[at[m]],
+            lambda m: (plan_ref[0, at[m]], plan_ref[1, at[m]]),
+            lambda m: plan_ref[2, at[m]],
             pages_ref,
         ).reshape(chunk, 16, HEAD_WIDTH)
         for m in range(chunk):
-            mixed_send[c * chunk + m] = jnp.where(length_ref[at[m]] > 0, mixed[m], 0.0).astype(
+            mixed_send[c * chunk + m] = jnp.where(plan_ref[2, at[m]] > 0, mixed[m], 0.0).astype(
                 jnp.bfloat16
             )
 
-        @pl.loop(c * chunk, (c + 1) * chunk)
-        def _(k):
-            @pl.when(k > 0)
-            def _():
-                pltpu.make_async_remote_copy(
-                    mixed_send.at[k],
-                    out_ref.at[resident + me],
-                    send_sem.at[6],
-                    one_sem.at[2],
-                    device_id={"pool": partner(k, 1)},
-                    device_id_type=MESH,
-                ).start()
+        def send_mixed(k, to):
+            pltpu.make_async_remote_copy(
+                mixed_send.at[k],
+                out_ref.at[resident + me],
+                send_sem.at[6],
+                one_sem.at[2],
+                device_id={"pool": to},
+                device_id_type=MESH,
+            ).start()
+
+        to_chunk(c, 1, send_mixed)
 
     pltpu.make_async_copy(
-        mixed_send.at[0], out_ref.at[resident + me], one_sem.at[2]
+        mixed_send.at[self_k], out_ref.at[resident + me], one_sem.at[2]
     ).start()
 
     others = pl.ds(0, groups - 1)
@@ -474,25 +537,21 @@
     resident = resident_length.shape[0]
     block = PER_OWNER * steps
     lines = heads * steps
-    chunk = min(CHUNK, groups)
+    chunk = 2 * groups // Z_CHIPS
     chunks = groups // chunk
-
-    group_ids = jnp.arange(groups, dtype=jnp.int32)
-    meant = prefill_target_group[:, None] == group_ids[None, :]
-    page0 = jnp.sum(jnp.where(meant, prefill_page_table[:, 0:1], 0), axis=0)
-    page1 = jnp.sum(jnp.where(meant, prefill_page_table[:, 1:2], 0), axis=0)
-    length = jnp.sum(jnp.where(meant, prefill_length[:, None], 0), axis=0)
+    most = max(chunk, resident) * lines
+
     base = (
         base_query_projection.reshape(slots, steps, heads, HEAD_WIDTH)
         .transpose(0, 2, 1, 3)
         .reshape(slots, lines, HEAD_WIDTH)
     )
     operands = [
-        page0,
-        page1,
-        length,
-        resident_page_table,
+        prefill_target_group,
+        prefill_length,
+        prefill_page_table.T,
         resident_length,
+        resident_page_table.T,
         request_adapter.reshape(1, slots),
         adapter_store_row.reshape(1, -1),
         tokens.reshape(slots * steps, width),
@@ -503,19 +562,19 @@
         prefill_page_pool,
         resident_page_pool,
     ]
-    smem = pl.BlockSpec(memory_space=pltpu.SMEM)
-    vmem = pl.BlockSpec(memory_space=pltpu.VMEM)
     hbm = pl.BlockSpec(memory_space=pl.ANY)
     half = jnp.bfloat16
     dma = pltpu.SemaphoreType.DMA
     out = pl.pallas_call(
         kernel,
         out_shape=jax.ShapeDtypeStruct((slots, lines, HEAD_WIDTH), half),
-        in_specs=[smem] * 5 + [vmem] * 3 + [hbm] * 6,
+        in_specs=[hbm] * len(operands),
         out_specs=hbm,
         scratch_shapes=[
-            pltpu.VMEM(operand.shape, half) for operand in operands[8:]
+            pltpu.SMEM(operand.shape, operand.dtype) for operand in operands[:5]
         ]
+        + [pltpu.VMEM(operand.shape, operand.dtype) for operand in operands[5:]]
+        + [pltpu.VMEM((8, HEAD_WIDTH), jnp.int32), pltpu.SMEM((8, HEAD_WIDTH), jnp.int32)]
         + [
             pltpu.VMEM((slots * block, groups * 2 * block), half),
             pltpu.VMEM((groups, block, width), half),
@@ -531,10 +590,10 @@
             pltpu.VMEM((groups, lines, HEAD_WIDTH), half),
             pltpu.VMEM((groups, lines, HEAD_WIDTH), half),
             pltpu.VMEM((resident, lines, HEAD_WIDTH), half),
-            pltpu.VMEM((chunk * lines, HEAD_WIDTH), jnp.float32),
-            pltpu.VMEM((chunk * lines, HEAD_WIDTH), half),
-            pltpu.VMEM((chunk * lines, HEAD_WIDTH), jnp.float32),
-            dma((6,)),
+            pltpu.VMEM((most, HEAD_WIDTH), jnp.float32),
+            pltpu.VMEM((most, HEAD_WIDTH), half),
+            pltpu.VMEM((most, HEAD_WIDTH), jnp.float32),
+            dma((len(operands) + 1,)),
             dma((chunks,)),
             dma((chunks,)),
             dma((chunks,)),
@@ -543,7 +602,7 @@
             dma((7,)),
         ],
         compiler_params=pltpu.CompilerParams(
-            collective_id=0, has_side_effects=True, vmem_limit_bytes=48 * 1024 * 1024
+            collective_id=0, has_side_effects=True, vmem_limit_bytes=60 * 1024 * 1024
         ),
     )(*operands)
     return (

time: 86.8 us -> 74.3 us (0.86)
  local copies, waits for them, and re-layouts: 11.9 us -> 3.58 us
  Pallas kernels: 73.7 us -> 70.5 us
    unnamed x20 -> x1, local copies, waits for them, and re-layouts: 10.1 us -> 1.78 us
    pallas_call x1, Pallas kernels: 73.7 us -> 70.5 us  [body(): pl.pallas_call(kernel, out_shape=jax.ShapeDtypeStruct((slots, lines, HEAD...]
where the time goes in v3:
time: 74.3 us; the launch traced here: 74.1 us
  Pallas kernels  70.5 us (95%)
  local copies, waits for them, and re-layouts  3.58 us (5%)
    pallas_call x1, Pallas kernels, body(): pl.pallas_call(kernel, out_shape=jax.ShapeDtypeStruct((slots, lines, HEAD...  70.5 us
    reshape x1, local copies, waits for them, and re-layouts, body(): tokens.reshape(slots * steps, width)  1.8 us
    unnamed x1, local copies, waits for them, and re-layouts  1.78 us

profile of v3, /device:TPU:1, one launch (start us, length us, event | category | flops | bytes accessed | tf_op | source)
XLA Modules:
  0.0 74.1 jit_solution(5340169287461808825)
XLA Ops:
  0.0 1.8 %reshape.32.tokens_hbm = bf16[288,640]{1,0:T(8,128)(2,1)} reshape(bf16[72,4,640]{2,1,0:T(4,128)(2,1)} %param.21) | data formatting | bytes 737280 | tf_op jit(solution)/shard_map/reshape | solution.py:557
  1.8 70.5 %shard_map.136 = bf16[72,16,128]{2,1,0:T(8,128)(2,1)} custom-call(s32[32]{0:T(128)} %target_hbm.1, s32[32]{0:T(128)} %length_hbm.1, s32[2,32]{1,0:T(2,128)} %bitcast.23, s32[8]{0:T(128)} %own_length_hbm.1, s32[2,8]{1,0:T(2,128)} %bitcast.24, s32[1,72]{1,0:T(1,128)} %bitcast.25, s32[1,512]{1,0:T(1,128)} %bitcast.22, bf16[288,640]{1,0:T(8,128)(2,1)} %reshape.32.tokens_hbm, ...), custom_call_target="tpu_custom_call" | custom-call | tf_op jit(solution)/shard_map/pallas_call | solution.py:568
  72.3 1.8 %copy.18 = bf16[72,4,512]{2,1,0:T(4,128)(2,1)} copy(bf16[72,4,512]{2,1,0:T(4,128)(2,1)} %bitcast.17) | data formatting | bytes 589824

commit v4 on v3

--- a/solution.py
+++ b/solution.py
@@ -89,6 +89,7 @@
     chunk = 2 * x_chips * CORES
     chunks = groups // chunk
     turns = sorted(range(x_chips), key=lambda x: -min(x, x_chips - x))
+    width = z_chips * CORES
     last, self_m = chunks - 1, chunk - CORES
     self_k = last * chunk + self_m
     ahead = [lax.rem(my_x + x, x_chips) * (z_chips * CORES) for x in turns]
@@ -106,6 +107,26 @@
             for to_x in (ahead if sign > 0 else behind)
             for core in cores
         ]
+
+    wide_turns = [(n + 1) // 2 if n % 2 else (z_chips - n // 2) % z_chips for n in range(z_chips)]
+
+    def columns(c, sign):
+        to_x = lax.rem(my_x + (c if sign > 0 else x_chips - c), x_chips) * (z_chips * CORES)
+        return [
+            to_x + lax.rem(my_z + (z if sign > 0 else z_chips - z), z_chips) * CORES + core
+            for z in wide_turns
+            for core in cores
+        ]
+
+    def to_column(c, sign, send):
+        for m, to in enumerate(columns(c, sign)):
+            if m == 0:
+
+                @pl.when(c > 0)
+                def _():
+                    send(c * width, to)
+            else:
+                send(c * width + m, to)
 
     def to_chunk(c, sign, send):
         for m, to in enumerate(partners(c, sign)):
@@ -153,11 +174,12 @@
 
     to_all(1, greet)
 
-    @pl.loop(1, peers)
-    def _(j):
-        pl.semaphore_signal(
-            barrier, inc=1, device_id={"tp": lax.rem(row + j, peers)}, device_id_type=MESH
-        )
+    others_in_row = [
+        lax.rem(row + j, peers)
+        for j in sorted(range(1, peers), key=lambda j: -min(j, peers - j))
+    ]
+    for peer in others_in_row:
+        pl.semaphore_signal(barrier, inc=1, device_id={"tp": peer}, device_id_type=MESH)
 
     for load in loads[:3]:
         load.wait()
@@ -204,7 +226,7 @@
     place_wide = place_wide * steps + step_of.astype(jnp.float32)
     row_ids = lax.broadcasted_iota(jnp.int32, (groups * block, wide), 0).astype(jnp.float32)
     dispatch = jnp.where(row_ids == place_wide, 1.0, 0.0).astype(jnp.bfloat16)
-    outgoing = jnp.dot(dispatch, tokens_ref[...], preferred_element_type=jnp.float32)
+    outgoing = jnp.dot(dispatch, tokens_ref[...].reshape(wide, tokens_ref.shape[2]), preferred_element_type=jnp.float32)
     x_send[...] = outgoing.reshape(x_send.shape).astype(jnp.bfloat16)
 
     pl.semaphore_wait(barrier, groups - 1 + peers - 1)
@@ -227,11 +249,30 @@
             device_id_type=MESH,
         ).start()
 
-    to_all(-1, send_tokens)
-
-    pltpu.make_async_copy(x_send.at[me], x_recv.at[self_k], x_sem.at[last]).start()
-    pltpu.make_async_copy(pick_send.at[me], pick_recv.at[self_k], pick_sem.at[last]).start()
-
+    @pl.loop(0, x_chips)
+    def _(c):
+        to_column(c, -1, functools.partial(send_tokens, c))
+
+    pltpu.make_async_copy(x_send.at[me], x_recv.at[0], x_sem.at[0]).start()
+    pltpu.make_async_copy(pick_send.at[me], pick_recv.at[0], pick_sem.at[0]).start()
+
+    loads[11].wait()
+
+    def send_fresh(c, k, to):
+        pltpu.make_async_remote_copy(
+            fresh_ref.at[resident + to],
+            fresh_recv.at[k],
+            send_sem.at[4],
+            one_sem.at[1],
+            device_id={"pool": to},
+            device_id_type=MESH,
+        ).start()
+
+    to_all(-1, send_fresh)
+
+    pltpu.make_async_copy(
+        fresh_ref.at[resident + me], fresh_recv.at[self_k], one_sem.at[1]
+    ).start()
     for load in loads[3:8]:
         load.wait()
     group_lane = lax.broadcasted_iota(jnp.int32, (1, plan_line.shape[1]), 1)
@@ -270,7 +311,7 @@
     loads[8].wait()
     loads[9].wait()
     lanes = HEAD_WIDTH // rank
-    rows = chunk * block
+    rows = width * block
     tiles = stored // lanes
     lane = lax.broadcasted_iota(jnp.int32, (rows, HEAD_WIDTH), 1)
     lane_half = (lane // rank).astype(jnp.float32)
@@ -280,11 +321,11 @@
         pltpu.make_async_copy(ref, ref, sem).wait()
 
     def picked(c):
-        pick = pick_recv[pl.ds(c * chunk, chunk)]
-        return jnp.broadcast_to(pick, (chunk, block, HEAD_WIDTH)).reshape(rows, HEAD_WIDTH)
+        pick = pick_recv[pl.ds(c * width, width)]
+        return jnp.broadcast_to(pick, (width, block, HEAD_WIDTH)).reshape(rows, HEAD_WIDTH)
 
     def shrink_chunk(c):
-        here = pl.ds(c * chunk, chunk)
+        here = pl.ds(c * width, width)
         wait_for(x_recv.at[here], x_sem.at[c])
         wait_for(pick_recv.at[here], pick_sem.at[c])
         x = x_recv[here].reshape(rows, x_recv.shape[2])
@@ -304,14 +345,13 @@
             part_send.at[c], part_recv.at[c, row], part_sem.at[c]
         ).start()
 
-        @pl.loop(1, peers)
-        def _(j):
+        for peer in others_in_row:
             pltpu.make_async_remote_copy(
                 part_send.at[c],
                 part_recv.at[c, row],
                 send_sem.at[2],
                 part_sem.at[c],
-                device_id={"tp": lax.rem(row + j, peers)},
+                device_id={"tp": peer},
                 device_id_type=MESH,
             ).start()
 
@@ -328,11 +368,11 @@
             [jnp.where(pick == lane_half + tile * lanes, low, 0.0) for tile in range(tiles)], 1
         ).astype(jnp.bfloat16)
         delta = jnp.dot(spread, expand_ref[...], preferred_element_type=jnp.float32)
-        here = pl.ds(c * chunk, chunk)
+        here = pl.ds(c * width, width)
         for head in range(4):
             piece = delta[:, head * HEAD_WIDTH : (head + 1) * HEAD_WIDTH]
             delta_send[here, head * block : (head + 1) * block, :] = piece.reshape(
-                chunk, block, HEAD_WIDTH
+                width, block, HEAD_WIDTH
             ).astype(jnp.bfloat16)
 
         def send_delta(k, to):
@@ -345,35 +385,18 @@
                 device_id_type=MESH,
             ).start()
 
-        to_chunk(c, 1, send_delta)
+        to_column(c, 1, send_delta)
 
     shrink_chunk(0)
 
-    @pl.loop(1, chunks)
+    @pl.loop(1, x_chips)
     def _(c):
         shrink_chunk(c)
         expand_chunk(c - 1)
 
-    expand_chunk(chunks - 1)
-    pltpu.make_async_copy(delta_send.at[self_k], delta_recv.at[me], one_sem.at[0]).start()
-
-    loads[11].wait()
-
-    def send_fresh(c, k, to):
-        pltpu.make_async_remote_copy(
-            fresh_ref.at[resident + to],
-            fresh_recv.at[k],
-            send_sem.at[4],
-            one_sem.at[1],
-            device_id={"pool": to},
-            device_id_type=MESH,
-        ).start()
-
-    to_all(-1, send_fresh)
-
-    pltpu.make_async_copy(
-        fresh_ref.at[resident + me], fresh_recv.at[self_k], one_sem.at[1]
-    ).start()
+    expand_chunk(x_chips - 1)
+    pltpu.make_async_copy(delta_send.at[0], delta_recv.at[me], one_sem.at[0]).start()
+
     loads[10].wait()
     loads[12].wait()
     loads[13].wait()
@@ -539,6 +562,7 @@
     lines = heads * steps
     chunk = 2 * groups // Z_CHIPS
     chunks = groups // chunk
+    columns = groups // (Z_CHIPS * CORES)
     most = max(chunk, resident) * lines
 
     base = (
@@ -554,7 +578,7 @@
         resident_page_table.T,
         request_adapter.reshape(1, slots),
         adapter_store_row.reshape(1, -1),
-        tokens.reshape(slots * steps, width),
+        tokens,
         shrink_weight.reshape(stored * rank, width),
         expand_weight.reshape(stored * rank, out_width),
         base,
@@ -581,8 +605,8 @@
             pltpu.VMEM((groups, block, width), half),
             pltpu.VMEM((groups, 1, HEAD_WIDTH), jnp.float32),
             pltpu.VMEM((groups, 1, HEAD_WIDTH), jnp.float32),
-            pltpu.VMEM((chunks, chunk * block // 2, HEAD_WIDTH), half),
-            pltpu.VMEM((chunks, peers, chunk * block // 2, HEAD_WIDTH), half),
+            pltpu.VMEM((columns, groups // columns * block // 2, HEAD_WIDTH), half),
+            pltpu.VMEM((columns, peers, groups // columns * block // 2, HEAD_WIDTH), half),
             pltpu.VMEM((groups, heads * block, HEAD_WIDTH), half),
             pltpu.VMEM((groups, heads * block, HEAD_WIDTH), half),
             pltpu.VMEM((groups, 2 * steps, HEAD_WIDTH), half),
@@ -594,9 +618,9 @@
             pltpu.VMEM((most, HEAD_WIDTH), half),
             pltpu.VMEM((most, HEAD_WIDTH), jnp.float32),
             dma((len(operands) + 1,)),
-            dma((chunks,)),
-            dma((chunks,)),
-            dma((chunks,)),
+            dma((columns,)),
+            dma((columns,)),
+            dma((columns,)),
             dma((chunks,)),
             dma((4,)),
             dma((7,)),

time: 74.3 us -> 69.6 us (0.937)
  Pallas kernels: 70.5 us -> 67.6 us
  local copies, waits for them, and re-layouts: 3.58 us -> 1.78 us
    pallas_call x1, Pallas kernels: 70.5 us -> 67.6 us  [body(): pl.pallas_call(kernel, out_shape=jax.ShapeDtypeStruct((slots, lines, HEAD...]
    reshape x1 -> x0, local copies, waits for them, and re-layouts: 1.8 us -> none  [body(): tokens.reshape(slots * steps, width)]
where the time goes in v4:
time: 69.6 us; the launch traced here: 69.4 us
  Pallas kernels  67.6 us (97%)
  local copies, waits for them, and re-layouts  1.78 us (3%)
    pallas_call x1, Pallas kernels, body(): pl.pallas_call(kernel, out_shape=jax.ShapeDtypeStruct((slots, lines, HEAD...  67.6 us
    unnamed x1, local copies, waits for them, and re-layouts  1.78 us

profile of v4, /device:TPU:1, one launch (start us, length us, event | category | flops | bytes accessed | tf_op | source)
XLA Modules:
  0.0 69.4 jit_solution(16890778263837395533)
XLA Ops:
  0.0 67.6 %shard_map.136 = bf16[72,16,128]{2,1,0:T(8,128)(2,1)} custom-call(s32[32]{0:T(128)} %target_hbm.1, s32[32]{0:T(128)} %length_hbm.1, s32[2,32]{1,0:T(2,128)} %bitcast.23, s32[8]{0:T(128)} %own_length_hbm.1, s32[2,8]{1,0:T(2,128)} %bitcast.24, s32[1,72]{1,0:T(1,128)} %bitcast.25, s32[1,512]{1,0:T(1,128)} %bitcast.22, bf16[72,4,640]{2,1,0:T(4,128)(2,1)} %tokens_hbm.1, ...), custom_call_target="tpu_custom_call" | custom-call | tf_op jit(solution)/shard_map/pallas_call | solution.py:592
  67.6 1.8 %copy.18 = bf16[72,4,512]{2,1,0:T(4,128)(2,1)} copy(bf16[72,4,512]{2,1,0:T(4,128)(2,1)} %bitcast.17) | data formatting | bytes 589824

commit v5 on v4

--- a/solution.py
+++ b/solution.py
@@ -90,6 +90,7 @@
     chunks = groups // chunk
     turns = sorted(range(x_chips), key=lambda x: -min(x, x_chips - x))
     width = z_chips * CORES
+    own_k = (x_chips - 1) * width
     last, self_m = chunks - 1, chunk - CORES
     self_k = last * chunk + self_m
     ahead = [lax.rem(my_x + x, x_chips) * (z_chips * CORES) for x in turns]
@@ -108,10 +109,11 @@
             for core in cores
         ]
 
-    wide_turns = [(n + 1) // 2 if n % 2 else (z_chips - n // 2) % z_chips for n in range(z_chips)]
+    wide_turns = [0] + sorted(range(1, z_chips), key=lambda z: -min(z, z_chips - z))
 
     def columns(c, sign):
-        to_x = lax.rem(my_x + (c if sign > 0 else x_chips - c), x_chips) * (z_chips * CORES)
+        x = x_chips - 1 - c
+        to_x = lax.rem(my_x + (x if sign > 0 else x_chips - x), x_chips) * (z_chips * CORES)
         return [
             to_x + lax.rem(my_z + (z if sign > 0 else z_chips - z), z_chips) * CORES + core
             for z in wide_turns
@@ -122,7 +124,7 @@
         for m, to in enumerate(columns(c, sign)):
             if m == 0:
 
-                @pl.when(c > 0)
+                @pl.when(c < x_chips - 1)
                 def _():
                     send(c * width, to)
             else:
@@ -142,6 +144,20 @@
         @pl.loop(0, chunks)
         def _(c):
             to_chunk(c, sign, functools.partial(send, c))
+
+    barrier = pltpu.get_barrier_semaphore()
+
+    def greet(c, k, to):
+        pl.semaphore_signal(barrier, inc=1, device_id={"pool": to}, device_id_type=MESH)
+
+    to_all(1, greet)
+
+    others_in_row = [
+        lax.rem(row + j, peers)
+        for j in sorted(range(1, peers), key=lambda j: -min(j, peers - j))
+    ]
+    for peer in others_in_row:
+        pl.semaphore_signal(barrier, inc=1, device_id={"tp": peer}, device_id_type=MESH)
 
     loads = [
         pltpu.make_async_copy(source, target, load_sem.at[n])
@@ -167,20 +183,6 @@
     for load in loads:
         load.start()
 
-    barrier = pltpu.get_barrier_semaphore()
-
-    def greet(c, k, to):
-        pl.semaphore_signal(barrier, inc=1, device_id={"pool": to}, device_id_type=MESH)
-
-    to_all(1, greet)
-
-    others_in_row = [
-        lax.rem(row + j, peers)
-        for j in sorted(range(1, peers), key=lambda j: -min(j, peers - j))
-    ]
-    for peer in others_in_row:
-        pl.semaphore_signal(barrier, inc=1, device_id={"tp": peer}, device_id_type=MESH)
-
     for load in loads[:3]:
         load.wait()
 
@@ -253,8 +255,8 @@
     def _(c):
         to_column(c, -1, functools.partial(send_tokens, c))
 
-    pltpu.make_async_copy(x_send.at[me], x_recv.at[0], x_sem.at[0]).start()
-    pltpu.make_async_copy(pick_send.at[me], pick_recv.at[0], pick_sem.at[0]).start()
+    pltpu.make_async_copy(x_send.at[me], x_recv.at[own_k], x_sem.at[x_chips - 1]).start()
+    pltpu.make_async_copy(pick_send.at[me], pick_recv.at[own_k], pick_sem.at[x_chips - 1]).start()
 
     loads[11].wait()
 
@@ -395,7 +397,7 @@
         expand_chunk(c - 1)
 
     expand_chunk(x_chips - 1)
-    pltpu.make_async_copy(delta_send.at[0], delta_recv.at[me], one_sem.at[0]).start()
+    pltpu.make_async_copy(delta_send.at[own_k], delta_recv.at[me], one_sem.at[0]).start()
 
     loads[10].wait()
     loads[12].wait()

time: 69.6 us -> 67.7 us (0.973)
  Pallas kernels: 67.6 us -> 65.8 us
    pallas_call x1, Pallas kernels: 67.6 us -> 65.8 us  [body(): pl.pallas_call(kernel, out_shape=jax.ShapeDtypeStruct((slots, lines, HEAD...]
where the time goes in v5:
time: 67.7 us; the launch traced here: 67.5 us
  Pallas kernels  65.8 us (97%)
  local copies, waits for them, and re-layouts  1.78 us (3%)
    pallas_call x1, Pallas kernels, body(): pl.pallas_call(kernel, out_shape=jax.ShapeDtypeStruct((slots, lines, HEAD...  65.8 us
    unnamed x1, local copies, waits for them, and re-layouts  1.78 us

profile of v5, /device:TPU:1, one launch (start us, length us, event | category | flops | bytes accessed | tf_op | source)
XLA Modules:
  0.0 67.5 jit_solution(86538736113238867)
XLA Ops:
  0.0 65.8 %shard_map.136 = bf16[72,16,128]{2,1,0:T(8,128)(2,1)} custom-call(s32[32]{0:T(128)} %target_hbm.1, s32[32]{0:T(128)} %length_hbm.1, s32[2,32]{1,0:T(2,128)} %bitcast.23, s32[8]{0:T(128)} %own_length_hbm.1, s32[2,8]{1,0:T(2,128)} %bitcast.24, s32[1,72]{1,0:T(1,128)} %bitcast.25, s32[1,512]{1,0:T(1,128)} %bitcast.22, bf16[72,4,640]{2,1,0:T(4,128)(2,1)} %tokens_hbm.1, ...), custom_call_target="tpu_custom_call" | custom-call | tf_op jit(solution)/shard_map/pallas_call | solution.py:594
  65.8 1.8 %copy.18 = bf16[72,4,512]{2,1,0:T(4,128)(2,1)} copy(bf16[72,4,512]{2,1,0:T(4,128)(2,1)} %bitcast.17) | data formatting | bytes 589824
